TPU v7x, 32 devices: a whole 2x2x4 slice. The times are simulated.
32 devices in a mesh: dp: 8 (over z, x), tensor: 4 (over y, core).
Axes of the slice: x: 2, y: 2, z: 4, core: 2. Of those that a mesh axis runs over, the one named last changes fastest.
Arguments:
- residual: bfloat16 [8, 2048, 1024], P('dp', 'tensor')
- teacher: bfloat16 [8, 2048, 1024], P('dp', 'tensor'), may hold values from -6 to 6
- valid_mask: int32 [8, 2048], P('dp', 'tensor'), may hold values from 0 to 1, as said below
- gain_in: float32 [1024], replicated, may hold values from 0.1 to 1.9
- w_z: bfloat16 [1024, 2048], P('dp', 'tensor'), may hold values from -0.1875 to 0.1875
- w_x: bfloat16 [1024, 2048], P('dp', 'tensor')
- w_bc: bfloat16 [1024, 256], P('dp'), may hold values from -0.1875 to 0.1875
- w_dt: bfloat16 [1024, 32], P('dp', 'tensor'), may hold values from -0.1875 to 0.1875
- conv_x: float32 [4, 2048], P(None, 'tensor'), may hold values from -3 to 3
- conv_bc: float32 [4, 256], replicated, may hold values from -3 to 3
- dt_bias: float32 [32], P('tensor'), may hold values from -6 to -2
- a_log: float32 [32], P('tensor'), may hold values from 0 to 2.77
- d_skip: float32 [32], P('tensor'), may hold values from 0.5 to 1.5
- gain_gate: float32 [2048], P('tensor'), may hold values from 0.1 to 1.9
- w_out: bfloat16 [1024, 2048], P('dp', 'tensor'), may hold values from -0.125 to 0.125
Outputs:
- mixed: bfloat16 [8, 2048, 1024], P('dp', 'tensor')
- loss: float32 [], replicated
- grad_residual: bfloat16 [8, 2048, 1024], P('dp', 'tensor')
- grad_gain_in: float32 [1024], replicated
- grad_w_z: float32 [1024, 2048], P('dp', 'tensor')
- grad_w_x: float32 [1024, 2048], P('dp', 'tensor')
- grad_w_bc: float32 [1024, 256], P('dp')
- grad_w_dt: float32 [1024, 32], P('dp', 'tensor')
- grad_conv_x: float32 [4, 2048], P(None, 'tensor')
- grad_conv_bc: float32 [4, 256], replicated
- grad_dt_bias: float32 [32], P('tensor')
- grad_a_log: float32 [32], P('tensor')
- grad_d_skip: float32 [32], P('tensor')
- grad_gain_gate: float32 [2048], P('tensor')
- grad_w_out: float32 [1024, 2048], P('dp', 'tensor')
Inputs may be any that keep to these rules, and one draw needn't show every extreme that they name: `valid_mask`: 1 marks a token that counts in the loss; the first token of every sequence counts.
All inputs are finite; a program needn't handle non-finite values.
Results may differ from a plain program's by a relative error of at most 0.011.
Values may be sent and summed in bfloat16 or wider, within the bound.
No kernel may reach another device: no remote copies, remote signals or barrier semaphores. Data moves between devices by JAX's collectives and lax.ppermute only.
A program may use at most 192 MiB of HBM per device.

v0:
```python
import jax
import jax.numpy as jnp
from jax import lax
from jax.sharding import PartitionSpec as P

HP = 64
BLOCK = 256


EPSILON = 1e-05
HIGH = lax.Precision.HIGHEST


def mat_mul(left_mat, right_mat):
    return jnp.dot(left_mat, right_mat, preferred_element_type=jnp.float32)


def mul_trans(left_mat, right_mat):
    return lax.dot_general(
        left_mat, right_mat, (((1,), (1,)), ((), ())), preferred_element_type=jnp.float32
    )


def mul_trans_hi(left_mat, right_mat):
    return lax.dot_general(
        left_mat,
        right_mat,
        (((1,), (1,)), ((), ())),
        precision=HIGH,
        preferred_element_type=jnp.float32,
    )


def trans_mul(left_mat, right_mat):
    return lax.dot_general(
        left_mat, right_mat, (((0,), (0,)), ((), ())), preferred_element_type=jnp.float32
    )


def trans_mul_hi(left_mat, right_mat):
    return lax.dot_general(
        left_mat,
        right_mat,
        (((0,), (0,)), ((), ())),
        precision=HIGH,
        preferred_element_type=jnp.float32,
    )


def prenorm(values, gain_vec):
    return (
        values * lax.rsqrt(jnp.mean(values * values, axis=-1, keepdims=True) + EPSILON) * gain_vec
    )


def convolve(values, kernel):
    taps = kernel.shape[0]
    length = values.shape[1]
    padded = jnp.pad(values, ((0, 0), (taps - 1, 0), (0, 0)))
    summed = padded[:, 0:length] * kernel[0]
    for offset in range(1, taps):
        summed = summed + padded[:, offset : offset + length] * kernel[offset]
    return jax.nn.silu(summed)


def conv_pair(inner_in, bc_in, conv_x, conv_bc):
    return (convolve(inner_in, conv_x), convolve(bc_in, conv_bc))


def scan_heads(inputs, steps_dt, rates, b_proj, c_proj, block):
    length, n_heads, head_dim = inputs.shape
    n_blocks = length // block
    x_blocks = inputs.reshape(n_blocks, block, n_heads, head_dim)
    dt_blocks = steps_dt.reshape(n_blocks, block, n_heads)
    b_blocks = b_proj.reshape(n_blocks, block, b_proj.shape[-1])
    c_blocks = c_proj.reshape(n_blocks, block, c_proj.shape[-1])
    lower_tri = (jnp.arange(block)[:, None] >= jnp.arange(block)[None, :])[None]

    def advance(carried, pieces):
        x_now, dt_now, b_now, c_now = pieces
        cum_rate = jnp.cumsum(dt_now * rates, axis=0).T
        spread_ts = cum_rate[:, :, None] - cum_rate[:, None, :]
        weights = jnp.where(lower_tri, jnp.exp(jnp.where(lower_tri, spread_ts, 0.0)), 0.0)
        scores = jnp.dot(c_now, b_now.T, precision=HIGH)
        mixing = weights * scores[None] * dt_now.T[:, None, :]
        inner_part = jnp.einsum("hts,shp->thp", mixing, x_now, precision=HIGH)
        carried_part = (
            jnp.einsum("tn,hpn->thp", c_now, carried, precision=HIGH)
            * jnp.exp(cum_rate).T[:, :, None]
        )
        tail_w = jnp.exp(cum_rate[:, -1:] - cum_rate).T * dt_now
        fresh_state = jnp.einsum("shp,sn->hpn", x_now * tail_w[:, :, None], b_now, precision=HIGH)
        carried = carried * jnp.exp(cum_rate[:, -1])[:, None, None] + fresh_state
        return (carried, inner_part + carried_part)

    start_state = jnp.zeros((n_heads, head_dim, b_proj.shape[-1]), jnp.float32)
    _, outputs = lax.scan(
        jax.checkpoint(advance), start_state, (x_blocks, dt_blocks, b_blocks, c_blocks)
    )
    return outputs.reshape(length, n_heads, head_dim)


def ssd_mixer(conv_x_out, conv_bc_out, gate_in, dt_in, dt_bias, a_log, d_skip):
    n_seqs, length, chans = conv_x_out.shape
    n_heads = chans // HP
    n_state = conv_bc_out.shape[-1] // 2
    steps_dt = jax.nn.softplus(dt_in + dt_bias)
    rates = -jnp.exp(a_log)
    heads_in = conv_x_out.reshape(n_seqs, length, n_heads, HP)

    def one_seq(seq_x, seq_dt, seq_b, seq_c):
        return scan_heads(seq_x, seq_dt, rates, seq_b, seq_c, BLOCK)

    scanned = jax.vmap(one_seq)(
        heads_in, steps_dt, conv_bc_out[..., :n_state], conv_bc_out[..., n_state:]
    )
    scanned = scanned + d_skip[:, None] * heads_in
    return scanned.reshape(n_seqs, length, chans) * jax.nn.silu(gate_in)


def rounded(values):
    return lax.optimization_barrier(values.astype(jnp.bfloat16)).astype(jnp.float32)


def spread_out(values, place, copies, axis):
    shape_full = list(values.shape)
    shape_full[axis] = shape_full[axis] * copies
    return lax.dynamic_update_slice_in_dim(
        jnp.zeros(shape_full, jnp.float32), values, place * values.shape[axis], axis
    )


def take_own(values, place, n_own, axis):
    return lax.dynamic_slice_in_dim(values, place * n_own, n_own, axis)


def body(
    residual,
    teacher,
    valid_mask,
    gain_in,
    w_z,
    w_x,
    w_bc,
    w_dt,
    conv_x,
    conv_bc,
    dt_bias,
    a_log,
    d_skip,
    gain_gate,
    w_out,
):
    n_seqs, pos_dev, width = residual.shape
    n_tensor = lax.axis_size("tensor")
    length = pos_dev * n_tensor
    tokens_all = n_seqs * length * lax.axis_size("dp")
    rows_all = n_seqs * length
    channels = w_z.shape[1]
    n_heads = w_dt.shape[1]
    bc_width = w_bc.shape[1]
    slab_rows = w_z.shape[0]
    inner_width = channels * n_tensor
    tensor_pos = lax.axis_index("tensor")
    valid = valid_mask.astype(jnp.float32)
    count = lax.psum(jnp.sum(valid), ("dp", "tensor"))
    upper = residual.astype(jnp.float32)
    normed, norm_pull = jax.vjp(prenorm, upper, gain_in)
    normed_low = normed.astype(jnp.bfloat16)
    gathered = lax.all_gather(normed_low, "tensor", axis=1, tiled=True)
    tok_rows = gathered.reshape(rows_all, width)
    pieces = (
        lax.all_gather(w_z, "dp", axis=0, tiled=True),
        lax.all_gather(w_x, "dp", axis=0, tiled=True),
        lax.all_gather(w_dt, "dp", axis=0, tiled=True),
        lax.all_gather(w_bc, "dp", axis=0, tiled=True),
    )
    columns = tok_rows
    gate_flat, inner_flat, dt_flat, bc_flat = tuple(
        (mat_mul(columns, w_piece) for w_piece in pieces)
    )
    gate_in = gate_flat.reshape(n_seqs, length, channels)
    inner_in = inner_flat.reshape(n_seqs, length, channels)
    dt_in = dt_flat.reshape(n_seqs, length, n_heads)
    bc_in = bc_flat.reshape(n_seqs, length, bc_width)
    (conv_x_out, conv_bc_out), conv_pull = jax.vjp(conv_pair, inner_in, bc_in, conv_x, conv_bc)
    conv_x_low = rounded(conv_x_out)
    conv_bc_low = rounded(conv_bc_out)
    gated, mixer_pull = jax.vjp(
        ssd_mixer, conv_x_low, conv_bc_low, gate_in, dt_in, dt_bias, a_log, d_skip
    )
    square_sums = lax.psum(jnp.sum(gated * gated, axis=-1), "tensor")
    norm_factor = lax.rsqrt(square_sums / inner_width + EPSILON)[..., None]
    normed_gate = (gated * norm_factor * gain_gate).astype(jnp.bfloat16)
    gate_rows = normed_gate.reshape(rows_all, channels)
    branch_part = mul_trans(gate_rows, lax.all_gather(w_out, "dp", axis=0, tiled=True))
    branch = lax.psum_scatter(
        branch_part.reshape(n_seqs, length, width), "tensor", scatter_dimension=1, tiled=True
    )
    result = upper + branch
    mixed = result.astype(jnp.bfloat16)
    error = result - teacher.astype(jnp.float32)
    loss_part = jnp.sum(valid[..., None] * error * error)
    grad_result = valid[..., None] * error * (tokens_all / count)
    grad_low = grad_result.astype(jnp.bfloat16)
    grad_rows = lax.all_gather(grad_low, "tensor", axis=1, tiled=True).reshape(rows_all, width)
    columns = grad_rows
    grad_gate_norm = mat_mul(columns, lax.all_gather(w_out, "dp", axis=0, tiled=True))
    grad_w_out_full = trans_mul(grad_rows, gate_rows)
    grad_gate_norm = grad_gate_norm.reshape(n_seqs, length, channels)
    prod_sums = lax.psum(jnp.sum(grad_gate_norm * gain_gate * gated, axis=-1), "tensor")
    grad_gated = (
        grad_gate_norm * gain_gate * norm_factor
        - gated * norm_factor**3 * (prod_sums / inner_width)[..., None]
    )
    grad_gain_gate = jnp.sum(grad_gate_norm * gated * norm_factor, axis=(0, 1))
    (
        grad_conv_x_out,
        grad_conv_bc_out,
        grad_gate_in,
        grad_dt_in,
        grad_dt_bias,
        grad_a_log,
        grad_d_skip,
    ) = mixer_pull(grad_gated)
    grad_inner_in, grad_bc_in, grad_conv_x, grad_conv_bc = conv_pull(
        (grad_conv_x_out, grad_conv_bc_out)
    )
    gate_grad_seq = grad_gate_in.astype(jnp.bfloat16)
    inner_grad_seq = grad_inner_in.astype(jnp.bfloat16)
    dt_grad_seq = grad_dt_in.astype(jnp.bfloat16)
    gate_grad_low = gate_grad_seq.reshape(rows_all, channels)
    inner_grad_low = inner_grad_seq.reshape(rows_all, channels)
    dt_grad_low = dt_grad_seq.reshape(rows_all, n_heads)
    bc_grad_rows = grad_bc_in.reshape(rows_all, bc_width)
    pieces = lax.all_gather((w_z, w_x, w_dt, w_bc), "dp", axis=0, tiled=True)
    back_rows = (
        mul_trans(gate_grad_low, pieces[0])
        + mul_trans(inner_grad_low, pieces[1])
        + mul_trans(dt_grad_low, pieces[2])
        + mul_trans_hi(bc_grad_rows, pieces[3].astype(jnp.float32))
    )
    grad_normed = lax.psum_scatter(
        back_rows.reshape(n_seqs, length, width), "tensor", scatter_dimension=1, tiled=True
    )
    grad_upper, grad_gain_part = norm_pull(grad_normed)
    grad_residual = (grad_result + grad_upper).astype(jnp.bfloat16)
    grad_z_full = trans_mul(tok_rows, gate_grad_low)
    grad_x_full = trans_mul(tok_rows, inner_grad_low)
    grad_dt_full = trans_mul(tok_rows, dt_grad_low)
    grad_bc_full = trans_mul_hi(tok_rows.astype(jnp.float32), bc_grad_rows)
    grad_w_z, grad_w_x, grad_w_dt, grad_w_out = (
        lax.psum_scatter(grad_z_full, "dp", scatter_dimension=0, tiled=True),
        lax.psum_scatter(grad_x_full, "dp", scatter_dimension=0, tiled=True),
        lax.psum_scatter(grad_dt_full, "dp", scatter_dimension=0, tiled=True),
        lax.psum_scatter(grad_w_out_full, "dp", scatter_dimension=0, tiled=True),
    )
    summed = lax.psum(
        (
            loss_part,
            grad_gain_part,
            spread_out(grad_conv_x, tensor_pos, n_tensor, 1),
            grad_conv_bc,
            grad_bc_full,
            spread_out(grad_dt_bias, tensor_pos, n_tensor, 0),
            spread_out(grad_a_log, tensor_pos, n_tensor, 0),
            spread_out(grad_d_skip, tensor_pos, n_tensor, 0),
            spread_out(grad_gain_gate, tensor_pos, n_tensor, 0),
        ),
        ("dp", "tensor"),
    )
    loss = summed[0] / (count * width)
    grad_gain_in = summed[1]
    grad_conv_x_own = take_own(summed[2], tensor_pos, channels, 1)
    grad_conv_bc_all = summed[3]
    grad_w_bc = take_own(summed[4], lax.axis_index("dp"), slab_rows, 0)
    grad_dt_bias_own = take_own(summed[5], tensor_pos, n_heads, 0)
    grad_a_log_own = take_own(summed[6], tensor_pos, n_heads, 0)
    grad_d_skip_own = take_own(summed[7], tensor_pos, n_heads, 0)
    grad_gain_gate_own = take_own(summed[8], tensor_pos, channels, 0)
    return (
        mixed,
        loss,
        grad_residual,
        grad_gain_in,
        grad_w_z,
        grad_w_x,
        grad_w_bc,
        grad_w_dt,
        grad_conv_x_own,
        grad_conv_bc_all,
        grad_dt_bias_own,
        grad_a_log_own,
        grad_d_skip_own,
        grad_gain_gate_own,
        grad_w_out,
    )


def solution(mesh):
    return jax.shard_map(
        body,
        mesh=mesh,
        in_specs=(
            P("dp", "tensor", None),
            P("dp", "tensor", None),
            P("dp", "tensor"),
            P(),
            P("dp", "tensor"),
            P("dp", "tensor"),
            P("dp", None),
            P("dp", "tensor"),
            P(None, "tensor"),
            P(),
            P("tensor"),
            P("tensor"),
            P("tensor"),
            P("tensor"),
            P("dp", "tensor"),
        ),
        out_specs=(
            P("dp", "tensor", None),
            P(),
            P("dp", "tensor", None),
            P(),
            P("dp", "tensor"),
            P("dp", "tensor"),
            P("dp", None),
            P("dp", "tensor"),
            P(None, "tensor"),
            P(),
            P("tensor"),
            P("tensor"),
            P("tensor"),
            P("tensor"),
            P("dp", "tensor"),
        ),
        check_vma=False,
    )
```

profile of v0, /device:TPU:0, one launch (start us, length us, event | category | flops | bytes accessed | tf_op | source)
XLA Modules:
  0.0 1142.2 jit_solution(6475424082212026266)
XLA Ops:
  15.5 27.8 %all_gather.27 = bf16[1024,8]{0,1:T(8,128)(2,1)S(1)} all-gather(bf16[128,8]{0,1:T(8,128)(2,1)S(1)} %copy-done.57), channel_id=1, replica_groups=mesh['dp'=8,'tensor'=4] {'dp'}, dimensions={0}, use_global_device_ids=true | all-gather | bytes 18432 | tf_op jit(solution)/shard_map/all_gather | solution.py:175
  43.3 31.3 %all_gather.29 = bf16[1024,256]{1,0:T(8,128)(2,1)S(1)} all-gather(bf16[128,256]{1,0:T(8,128)(2,1)S(1)} %copy-done.23), channel_id=1, replica_groups=mesh['dp'=8,'tensor'=4] {'dp'}, dimensions={0}, use_global_device_ids=true | all-gather | bytes 589824 | tf_op jit(solution)/shard_map/all_gather | solution.py:176
  83.3 9.3 all-gather.8.cloned.1.call-done
  119.2 104.2 %while.44 = (s32[]{:T(128)}, f32[1,8,64,128]{3,2,1,0:T(8,128)S(1)}, f32[8,1,256,8,64]{2,4,3,1,0:T(8,128)}, f32[8,1,8,64,128]{4,3,2,1,0:T(8,128)}, f32[8,1,256,8]...) while((s32[]{:T(128)}, f32[1,8,64,128]{3,2,1,0:T(8,128)S(1)}, ...), condition=%wide.region_4.5_spmd.clone.clone, body=%wide.region_1.4_spmd.clone.clone.sunk | while | flops 909582336 | bytes 5206924 | solution.py:97
  223.4 7.3 copy.171
  230.7 7.9 reshape.1292
  238.6 10.4 multiply_reduce_fusion.10
  254.9 8.1 convolution_bitcast_fusion.7
  264.3 39.0 %psum.86 = f32[]{:T(128)} all-reduce(f32[]{:T(128)} %convert_reduce_fusion), channel_id=1, replica_groups=mesh['dp'=8,'tensor'=4] {'dp','tensor'}, use_global_device_ids=true, to_apply=%region_11.12 | all-reduce | flops 1 | bytes 8 | tf_op jit(solution)/shard_map/psum | solution.py:166
  304.0 30.7 %reduce-scatter.7.cloned.1.call-done = f32[1,512,1024]{2,1,0:T(8,128)} async-done(((f32[1,2048,1024]{2,1,0:T(8,128)}), f32[1,512,1024]{2,1,0:T(8,128)}) %reduce-scatter.7.cloned.1.call-update) | async-done | bytes 2097168 | tf_op jit(solution)/shard_map/reduce_scatter | solution.py:197
  338.1 34.5 %all-gather.14.cloned.1.call-done = bf16[1,2048,1024]{2,1,0:T(8,128)(2,1)} async-done(((bf16[1,512,1024]{2,1,0:T(8,128)(2,1)}), bf16[1,2048,1024]{2,1,0:T(8,128)(2,1)}) %all-gather.14.cloned.1.call-update) | async-done | bytes 4194320 | tf_op jit(solution)/shard_map/all_gather | solution.py:206
  372.6 9.1 multiply_reduce_fusion.4
  387.8 8.4 fusion.129
  421.5 219.1 %while.43 = (s32[]{:T(128)}, f32[8]{0:T(128)}, f32[1,8,64,128]{3,2,1,0:T(8,128)}, f32[8,1,256,8,64]{2,4,3,1,0:T(8,128)}, f32[8,1,256,8]{2,3,1,0:T(8,128)}, /*ind...) while((s32[]{:T(128)}, f32[8]{0:T(128)}, ...), condition=%wide.region_28.29_spmd.clone, body=%wide.region_14.28_spmd.clone.sunk | while | flops 2126557184 | bytes 15911476 | solution.py:97
  665.6 7.5 reshape.1294
  673.2 11.4 multiply_reduce_fusion.7
  709.0 10.9 add_bitcast_fusion
  723.6 7.3 fusion.134
  745.5 44.2 %all-reduce.25.cloned.1.call-done = f32[1024,256]{1,0:T(8,128)} async-done(((f32[1024,256]{1,0:T(8,128)}), f32[1024,256]{1,0:T(8,128)}) %all-reduce.25.cloned.1.call-update) | async-done | bytes 1048592 | tf_op jit(solution)/shard_map/psum | solution.py:258
  791.3 71.7 %reduce-scatter.9.cloned.1.call-done = f32[1,512,1024]{2,1,0:T(8,128)} async-done(((f32[1,2048,1024]{2,1,0:T(8,128)}), f32[1,512,1024]{2,1,0:T(8,128)}) %reduce-scatter.9.cloned.1.call-update) | async-done | bytes 2097168 | tf_op jit(solution)/shard_map/reduce_scatter | solution.py:243
  866.8 40.6 %all-reduce.22 = (f32[]{:T(128)}, f32[1024]{0:T(1024)}, f32[4,2048]{1,0:T(4,128)S(1)}, f32[4,256]{1,0:T(4,128)}, f32[32]{0:T(128)S(1)}, /*index=5*/f32[32]{0:T(128)S(1)}, f32[32]{0:T(128)S(1)}, f32[2048]{0:T(1024)S(1)}) all-reduce(f32[]{:T(128)} %get-tuple-element.728, ...), channel_id=1, replica_groups=mesh['dp'=8,'tensor'=4] {'dp','tensor'}, use_global_device_ids=true, to_apply=%region_9.10 | all-reduce | flops 12385 | bytes 99080 | tf_op jit(solution)/shard_map/psum | solution.py:258
  920.7 70.9 %reduce-scatter.17.cloned.1.call-done = f32[128,512]{1,0:T(8,128)} async-done(((f32[1024,512]{1,0:T(8,128)}), f32[128,512]{1,0:T(8,128)}) %reduce-scatter.17.cloned.1.call-update) | async-done | bytes 262160 | tf_op jit(solution)/shard_map/reduce_scatter | solution.py:256
  991.6 71.5 %reduce-scatter.11.cloned.1.call-done = f32[128,512]{1,0:T(8,128)} async-done(((f32[1024,512]{1,0:T(8,128)}), f32[128,512]{1,0:T(8,128)}) %reduce-scatter.11.cloned.1.call-update) | async-done | bytes 262160 | tf_op jit(solution)/shard_map/reduce_scatter | solution.py:253
  1063.0 71.0 %reduce-scatter.13.cloned.1.call-done = f32[128,512]{1,0:T(8,128)} async-done(((f32[1024,512]{1,0:T(8,128)}), f32[128,512]{1,0:T(8,128)}) %reduce-scatter.13.cloned.1.call-update) | async-done | bytes 262160 | tf_op jit(solution)/shard_map/reduce_scatter | solution.py:254
  (674 shorter events, 491.5 us)
Async XLA Ops:
  7.2 67.3 %all-gather.6.cloned.1.call-start = ((), (), s32[]{:S(2)}) async-start(), calls=%async_computation.6 | async-start | bytes 5242880 | tf_op jit(solution)/shard_map/all_gather | solution.py:170
  12.5 80.1 %all-gather.8.cloned.1.call-start = ((), (), s32[]{:S(2)}) async-start(), calls=%async_computation.7 | async-start | bytes 1179648 | tf_op jit(solution)/shard_map/all_gather | solution.py:174
  13.3 225.3 %all-gather.10.cloned.1.call-start = ((), (), s32[]{:S(2)}) async-start(), calls=%async_computation.8 | async-start | bytes 1179648 | tf_op jit(solution)/shard_map/all_gather | solution.py:173
  14.0 240.9 %all-gather.12.cloned.1.call-start = ((), (), s32[]{:S(2)}) async-start(), calls=%async_computation.9 | async-start | bytes 1179648 | tf_op jit(solution)/shard_map/all_gather | solution.py:196
  14.6 320.1 %reduce-scatter.7.cloned.1.call-start = ((), (), s32[]{:S(2)}) async-start(), calls=%async_computation.10 | async-start | bytes 10485760 | tf_op jit(solution)/shard_map/reduce_scatter | solution.py:197
  15.4 372.4 %copy-start.29 = (f32[512]{0:T(512)}, f32[512]{0:T(512)S(1)}, u32[]{:S(2)}) copy-start(f32[512]{0:T(512)S(1)} %mul.905) | copy-start | bytes 6148
  15.5 82.0 %copy-start.31 = (f32[1,512]{1,0:T(1,128)}, f32[1,512]{1,0:T(1,128)S(1)}, u32[]{:S(2)}) copy-start(f32[1,512]{1,0:T(1,128)S(1)} %get-tuple-element.823) | copy-start | bytes 6148
  15.5 82.0 %copy-start.33 = (f32[1,512]{1,0:T(1,128)}, f32[1,512]{1,0:T(1,128)S(1)}, u32[]{:S(2)}) copy-start(f32[1,512]{1,0:T(1,128)S(1)} %get-tuple-element.824) | copy-start | bytes 6148
  15.5 82.0 %copy-start.35 = (f32[1,512]{1,0:T(1,128)}, f32[1,512]{1,0:T(1,128)S(1)}, u32[]{:S(2)}) copy-start(f32[1,512]{1,0:T(1,128)S(1)} %get-tuple-element.825) | copy-start | bytes 6148
  15.5 82.0 %copy-start.37 = (f32[1,512]{1,0:T(1,128)}, f32[1,512]{1,0:T(1,128)S(1)}, u32[]{:S(2)}) copy-start(f32[1,512]{1,0:T(1,128)S(1)} %get-tuple-element.826) | copy-start | bytes 6148
  254.8 141.4 %copy-start.21 = (f32[1,2048]{1,0:T(1,128)}, f32[1,2048]{1,0:T(1,128)S(1)}, u32[]{:S(2)}) copy-start(f32[1,2048]{1,0:T(1,128)S(1)} %add_rsqrt_fusion) | copy-start | bytes 24580
  263.0 71.7 %copy-start.4 = (bf16[1,512,1024]{2,1,0:T(8,128)(2,1)S(1)}, bf16[1,512,1024]{2,1,0:T(8,128)(2,1)}, u32[]{:S(2)}) copy-start(bf16[1,512,1024]{2,1,0:T(8,128)(2,1)} %param.19) | copy-start | bytes 3145732
  263.0 109.6 %all-gather.14.cloned.1.call-start = ((), (), s32[]{:S(2)}) async-start(), calls=%async_computation.11 | async-start | bytes 5242880 | tf_op jit(solution)/shard_map/all_gather | solution.py:206
  338.0 451.7 %all-reduce.25.cloned.1.call-start = ((), (), s32[]{:S(2)}) async-start(), calls=%async_computation.15 | async-start | bytes 2097152 | tf_op jit(solution)/shard_map/psum | solution.py:258
  658.6 204.4 %reduce-scatter.9.cloned.1.call-start = ((), (), s32[]{:S(2)}) async-start(), calls=%async_computation.12 | async-start | bytes 10485760 | tf_op jit(solution)/shard_map/reduce_scatter | solution.py:243
  720.0 200.7 %reduce-scatter.15.cloned.1.call-start = ((), (), s32[]{:S(2)}) async-start(), calls=%async_computation.16 | async-start | bytes 36864 | tf_op jit(solution)/shard_map/reduce_scatter | solution.py:255
  723.5 268.0 %reduce-scatter.17.cloned.1.call-start = ((), (), s32[]{:S(2)}) async-start(), calls=%async_computation.17 | async-start | bytes 2359296 | tf_op jit(solution)/shard_map/reduce_scatter | solution.py:256
  730.9 332.1 %reduce-scatter.11.cloned.1.call-start = ((), (), s32[]{:S(2)}) async-start(), calls=%async_computation.13 | async-start | bytes 2359296 | tf_op jit(solution)/shard_map/reduce_scatter | solution.py:253
  737.0 126.1 %copy-start.5 = (f32[1,512,1024]{2,1,0:T(8,128)S(1)}, f32[1,512,1024]{2,1,0:T(8,128)}, u32[]{:S(2)}) copy-start(f32[1,512,1024]{2,1,0:T(8,128)} %reduce-scatter.7.cloned.1.call-done) | copy-start | bytes 6291460
  737.0 126.1 %copy-start.24 = (f32[1024]{0:T(1024)S(1)}, f32[1024]{0:T(1024)}, u32[]{:S(2)}) copy-start(f32[1024]{0:T(1024)} %param.22) | copy-start | bytes 12292
  737.0 126.1 %copy-start.26 = (f32[1,512]{1,0:T(1,128)S(1)}, f32[1,512]{1,0:T(1,128)}, u32[]{:S(2)}) copy-start(f32[1,512]{1,0:T(1,128)} %copy-done.25) | copy-start | bytes 6148
  737.0 126.0 %copy-start.28 = (f32[512]{0:T(512)S(1)}, f32[512]{0:T(512)}, u32[]{:S(2)}) copy-start(f32[512]{0:T(512)} %copy-done.27) | copy-start | bytes 6148
  737.0 397.1 %reduce-scatter.13.cloned.1.call-start = ((), (), s32[]{:S(2)}) async-start(), calls=%async_computation.14 | async-start | bytes 2359296 | tf_op jit(solution)/shard_map/reduce_scatter | solution.py:254
  743.7 167.4 %copy-start.40 = (f32[512]{0:T(512)S(1)}, f32[512]{0:T(512)}, u32[]{:S(2)}) copy-start(f32[512]{0:T(512)} %copy-done.39) | copy-start | bytes 6148
  (54 other events, 694.8 us)
Sparse Core Ops, SparseCore 0:
  12.6 37.1 all-gather.5
  52.0 40.5 all-gather.7
  94.8 38.9 all-gather.9
  135.7 38.9 all-gather.11
  263.1 71.4 reduce-scatter.6
  338.1 34.4 all-gather.13
  658.8 130.9 all-reduce.24
  792.3 70.6 reduce-scatter.8
  867.1 53.5 reduce-scatter.14
  925.0 66.4 reduce-scatter.16
  996.1 66.9 reduce-scatter.10
  1067.4 66.6 reduce-scatter.12
where the time goes:
time: 1150 us; the launch traced here: 1140 us
  waiting for transfers between devices  411 us (36%)
  matrix products  280 us (24%)
  other arithmetic  154 us (13%)
  blocking collectives  150 us (13%)
  local copies, waits for them, and re-layouts  126 us (11%)
  between operations  18.4 us (2%)
    dot_general x24, matrix products, advance(): inner_part = jnp.einsum('hts,shp->thp', mixing, x_now, precision=HIGH)  93.9 us
    reduce_scatter x1, waiting for transfers between devices, body(): lax.psum_scatter(back_rows.reshape(n_seqs, length, width), 'tensor', scat...  71.7 us
    reduce_scatter x1, waiting for transfers between devices, body(): lax.psum_scatter(grad_z_full, 'dp', scatter_dimension=0, tiled=True)  71.5 us
    reduce_scatter x1, waiting for transfers between devices, body(): lax.psum_scatter(grad_x_full, 'dp', scatter_dimension=0, tiled=True)  71 us
    reduce_scatter x1, waiting for transfers between devices, body(): lax.psum_scatter(grad_w_out_full, 'dp', scatter_dimension=0, tiled=True)  70.9 us
    psum x1, waiting for transfers between devices, body(): lax.psum((loss_part, grad_gain_part, spread_out(grad_conv_x, tensor_pos,...  44.2 us
    another operation x88, other arithmetic  43.8 us
    psum x1, blocking collectives, body(): lax.psum((loss_part, grad_gain_part, spread_out(grad_conv_x, tensor_pos,...  40.6 us
  transfers between devices with their start and end apart: 12, of which 9 were waited for; matrix products, arithmetic and copies ran while one was open for 23% of the time, Pallas kernels for 0%

commit v1 on v0

v1 whole, which is shorter than its diff:
```python
import functools

import jax
import jax.numpy as jnp
from jax import lax
from jax.experimental import pallas as pl
from jax.experimental.pallas import tpu as pltpu
from jax.sharding import PartitionSpec as P

HP = 64
BLOCK = 256
EPSILON = 1e-05
HEADS_PAD = 128
HALO = 16
BF = jnp.bfloat16
F32 = jnp.float32
HIGH = lax.Precision.HIGHEST
VMEM_LIMIT = 56 * 1024 * 1024
AXES = ("dp", "tensor")


def dot_nn(left, right):
    return lax.dot_general(left, right, (((1,), (0,)), ((), ())), preferred_element_type=F32)


def dot_nt(left, right):
    return lax.dot_general(left, right, (((1,), (1,)), ((), ())), preferred_element_type=F32)


def dot_tn(left, right):
    return lax.dot_general(left, right, (((0,), (0,)), ((), ())), preferred_element_type=F32)


def split_low(values):
    high = values.astype(BF)
    return high, (values - high.astype(F32)).astype(BF)


def by_expansion(values, spread_mat):
    high, rest = split_low(values)
    return dot_nn(high, spread_mat) + dot_nn(rest, spread_mat)


def per_head(values, spread_mat):
    high, rest = split_low(values)
    return dot_nt(high, spread_mat) + dot_nt(rest, spread_mat)


def sigmoid(values):
    return 1.0 / (1.0 + jnp.exp(-values))


def call(kernel, grid, in_specs, out_specs, out_shape, scratch=(), prefetch=0, flops=0, nbytes=0):
    return pl.pallas_call(
        kernel,
        grid_spec=pltpu.PrefetchScalarGridSpec(
            num_scalar_prefetch=prefetch,
            grid=grid,
            in_specs=in_specs,
            out_specs=out_specs,
            scratch_shapes=list(scratch),
        ),
        out_shape=out_shape,
        compiler_params=pltpu.CompilerParams(
            dimension_semantics=("arbitrary",) * len(grid), vmem_limit_bytes=VMEM_LIMIT
        ),
        cost_estimate=pl.CostEstimate(flops=flops, bytes_accessed=nbytes, transcendentals=0),
    )


def whole(shape):
    rank = len(shape)
    return pl.BlockSpec(shape, lambda *_: (0,) * rank, pipeline_mode=pl.Buffered(1))


def rows(block, width):
    return pl.BlockSpec((block, width), lambda i, *_: (i, 0))


def out(shape, dtype):
    return jax.ShapeDtypeStruct(shape, dtype)


def front_kernel(
    n_ref, halo_ref, wx_ref, wbc_ref, wdt_ref, cx_ref, cbc_ref, bias_ref, rate_ref, spread_ref,
    xin_ref, xc_ref, bcin_ref, bcc_ref, dt_ref, a_ref, ag_ref, sig_ref, at_ref, state_ref,
    xs, bs, before,
):
    step = pl.program_id(0)
    block = n_ref.shape[0]
    chans = wx_ref.shape[1]
    bcw = wbc_ref.shape[1]
    n_state = bcw // 2

    @pl.when(step == 0)
    def _():
        halo_x = dot_nn(halo_ref[...], wx_ref[...])
        halo_bc = dot_nn(halo_ref[...], wbc_ref[...])
        xs[0:8, :] = halo_x[8:16]
        bs[0:8, :] = halo_bc[8:16]
        before[...] = jnp.zeros_like(before)
        state_ref[...] = jnp.zeros_like(state_ref)

    @pl.when(step > 0)
    def _():
        xs[0:8, :] = xs[block : block + 8, :]
        bs[0:8, :] = bs[block : block + 8, :]

    n_now = n_ref[...]
    xs[8 : block + 8, :] = dot_nn(n_now, wx_ref[...])
    bs[8 : block + 8, :] = dot_nn(n_now, wbc_ref[...])
    xin_ref[...] = xs[8 : block + 8, :].astype(BF)
    bcin_ref[...] = bs[8 : block + 8, :].astype(BF)
    dt_raw = dot_nt(wdt_ref[...], n_now) + bias_ref[...]
    tail = jnp.exp(-jnp.abs(dt_raw))
    log_part = jnp.where(
        tail < 0.01, tail * (1.0 - tail * (0.5 - tail * (1.0 / 3.0))), jnp.log(1.0 + tail)
    )
    dt_t = jnp.maximum(dt_raw, 0.0) + log_part
    row_i = lax.broadcasted_iota(jnp.int32, (block, block), 0)
    col_i = lax.broadcasted_iota(jnp.int32, (block, block), 1)
    upto = jnp.where(row_i <= col_i, 1.0, 0.0).astype(F32)
    a_t = jnp.dot(dt_t * rate_ref[...], upto, precision=HIGH, preferred_element_type=F32)
    at_ref[...] = a_t[0 : at_ref.shape[0]]
    a_now = a_t.T
    dt_now = dt_t.T
    a_ref[...] = a_now
    dt_ref[...] = dt_now
    sig_ref[...] = sigmoid(dt_raw.T)
    ag_ref[...] = a_now + before[0:1]
    a_last = a_now[block - 1 : block]
    before[...] = before[...] + a_last
    for col in range(0, bcw, 128):
        pre = bs[5 : block + 5, col : col + 128] * cbc_ref[0:1, col : col + 128]
        for k in range(1, 4):
            pre += bs[5 + k : block + 5 + k, col : col + 128] * cbc_ref[k : k + 1, col : col + 128]
        bcc_ref[:, col : col + 128] = (pre * sigmoid(pre)).astype(BF)
    for col in range(0, chans, 128):
        pre = xs[5 : block + 5, col : col + 128] * cx_ref[0:1, col : col + 128]
        for k in range(1, 4):
            pre += xs[5 + k : block + 5 + k, col : col + 128] * cx_ref[k : k + 1, col : col + 128]
        xc_ref[:, col : col + 128] = (pre * sigmoid(pre)).astype(BF)
    spread = spread_ref[...]
    weight = by_expansion(dt_now * jnp.exp(a_last - a_now), spread)
    weighted = (xc_ref[...].astype(F32) * weight).astype(BF)
    decay = by_expansion(jnp.broadcast_to(jnp.exp(a_last), (8, HEADS_PAD)), spread)
    state_ref[...] = state_ref[...] * decay[0:1] + dot_tn(bcc_ref[:, 0:n_state], weighted)


def front(n_full, halo, wx, wbc, wdt, conv_x, conv_bc, bias, rate, spread):
    toks, width = n_full.shape
    chans = wx.shape[1]
    bcw = wbc.shape[1]
    n_state = bcw // 2
    heads = chans // HP
    nb = toks // BLOCK
    return call(
        front_kernel,
        (nb,),
        [
            rows(BLOCK, width), whole(halo.shape), whole(wx.shape), whole(wbc.shape),
            whole(wdt.shape), whole(conv_x.shape), whole(conv_bc.shape), whole(bias.shape),
            whole(rate.shape), whole(spread.shape),
        ],
        [
            rows(BLOCK, chans), rows(BLOCK, chans), rows(BLOCK, bcw), rows(BLOCK, bcw),
            rows(BLOCK, HEADS_PAD), rows(BLOCK, HEADS_PAD), rows(BLOCK, HEADS_PAD),
            rows(BLOCK, HEADS_PAD), pl.BlockSpec((heads, BLOCK), lambda i: (0, i)),
            whole((n_state, chans)),
        ],
        [
            out((toks, chans), BF), out((toks, chans), BF), out((toks, bcw), BF),
            out((toks, bcw), BF), out((toks, HEADS_PAD), F32), out((toks, HEADS_PAD), F32),
            out((toks, HEADS_PAD), F32), out((toks, HEADS_PAD), F32), out((heads, toks), F32),
            out((n_state, chans), F32),
        ],
        [
            pltpu.VMEM((BLOCK + 8, chans), F32), pltpu.VMEM((BLOCK + 8, bcw), F32),
            pltpu.VMEM((8, HEADS_PAD), F32),
        ],
        flops=2 * toks * width * (chans + bcw), nbytes=8 * toks * chans,
    )(n_full, halo, wx, wbc, wdt, conv_x, conv_bc, bias, rate, spread)


def scan_kernel(
    xc_ref, bcc_ref, dt_ref, a_ref, at_ref, start_ref, spread_ref, y_ref, saved_ref, xt, state
):
    step = pl.program_id(0)
    block, chans = xc_ref.shape
    n_state = bcc_ref.shape[1] // 2
    half = block // 2

    @pl.when(step == 0)
    def _():
        state[...] = start_ref[...].astype(F32)

    spread = spread_ref[...]
    b_now = bcc_ref[:, 0:n_state]
    c_now = bcc_ref[:, n_state:]
    a_now = a_ref[...]
    a_last = a_now[block - 1 : block]
    state_low = state[...].astype(BF)
    saved_ref[0] = state_low
    xt[...] = (xc_ref[...].astype(F32) * by_expansion(dt_ref[...], spread)).astype(BF)
    y_ref[...] = dot_nn(c_now, state_low) * by_expansion(jnp.exp(a_now), spread)
    scores = dot_nt(c_now, b_now)
    row_i = lax.broadcasted_iota(jnp.int32, (half, half), 0)
    col_i = lax.broadcasted_iota(jnp.int32, (half, half), 1)
    shut = jnp.where(row_i >= col_i, 0.0, -1e30).astype(F32)
    lane = lax.broadcasted_iota(jnp.int32, (half, 128), 1)
    for pair in range(chans // 128):
        cols = slice(pair * 128, pair * 128 + 128)
        x_pair = xt[:, cols]
        tops, lows = [], []
        for sub in range(2):
            h = pair * 2 + sub
            a_row = at_ref[h : h + 1, :]
            a_top = a_now[0:half, h : h + 1]
            a_low = a_now[half:block, h : h + 1]
            m_top = jnp.exp(a_top - a_row[:, 0:half] + shut) * scores[0:half, 0:half]
            m_left = jnp.exp(a_low - a_row[:, 0:half]) * scores[half:block, 0:half]
            m_low = jnp.exp(a_low - a_row[:, half:block] + shut) * scores[half:block, half:block]
            tops.append(dot_nn(m_top.astype(BF), x_pair[0:half]))
            lows.append(
                dot_nn(jnp.concatenate([m_left.astype(BF), m_low.astype(BF)], axis=1), x_pair)
            )
        y_ref[0:half, cols] += jnp.where(lane < HP, tops[0], tops[1])
        y_ref[half:block, cols] += jnp.where(lane < HP, lows[0], lows[1])
    tail = by_expansion(jnp.exp(a_last - a_now), spread)
    decay = by_expansion(jnp.broadcast_to(jnp.exp(a_last), (8, HEADS_PAD)), spread)
    state[...] = state[...] * decay[0:1] + dot_tn(
        b_now, (xt[...].astype(F32) * tail).astype(BF)
    )
    saved_ref[1] = state[...].astype(BF)


def scan_forward(xc, bcc, dt, a_cols, a_rows, start, spread):
    toks, chans = xc.shape
    bcw = bcc.shape[1]
    n_state = bcw // 2
    heads = chans // HP
    nb = toks // BLOCK
    return call(
        scan_kernel,
        (nb,),
        [
            rows(BLOCK, chans), rows(BLOCK, bcw), rows(BLOCK, HEADS_PAD), rows(BLOCK, HEADS_PAD),
            pl.BlockSpec((heads, BLOCK), lambda i: (0, i)), whole(start.shape),
            whole(spread.shape),
        ],
        [rows(BLOCK, chans), pl.BlockSpec((2, n_state, chans), lambda i: (i, 0, 0))],
        [out((toks, chans), F32), out((2 * nb, n_state, chans), BF)],
        [pltpu.VMEM((BLOCK, chans), BF), pltpu.VMEM((n_state, chans), F32)],
        flops=2 * toks * BLOCK * chans * 2, nbytes=10 * toks * chans,
    )(xc, bcc, dt, a_cols, a_rows, start, spread)


def gate_kernel(
    where_ref, n_ref, y_ref, xc_ref, wz_ref, wo_ref, skip_ref, gain_ref,
    gate_out, u_ref, far_ref, near_ref, sq_ref,
):
    step = pl.program_id(0)
    chans = y_ref.shape[1]
    n_now = n_ref[...]
    squares = jnp.zeros((n_now.shape[0], 128), F32)
    for col in range(0, chans, 256):
        cols = slice(col, col + 256)
        gate = dot_nn(n_now, wz_ref[:, cols])
        gated = (y_ref[:, cols] + skip_ref[:, cols] * xc_ref[:, cols].astype(F32)) * (
            gate * sigmoid(gate)
        )
        gate_out[:, cols] = gate.astype(BF)
        u_ref[:, cols] = (gated * gain_ref[:, cols]).astype(BF)
        sq = gated * gated
        squares += sq[:, 0:128] + sq[:, 128:256]
    sq_ref[...] = jnp.broadcast_to(jnp.sum(squares, axis=1, keepdims=True), squares.shape)
    part = dot_nt(u_ref[...], wo_ref[...])

    @pl.when(step < 2)
    def _():
        far_ref[...] = part.astype(BF)

    @pl.when(step >= 2)
    def _():
        near_ref[...] = part


def gate_out_proj(place, n_full, y, xc, wz, wo, skip_row, gain_row):
    toks, width = n_full.shape
    chans = wz.shape[1]
    nb = toks // BLOCK

    def spot(i, where):
        return (((i // 2) + 1 - where[3]) % 2) * 2 + i % 2

    def moved(w):
        return pl.BlockSpec((BLOCK, w), lambda i, where: (spot(i, where), 0))

    return call(
        gate_kernel,
        (nb,),
        [
            moved(width), moved(chans), moved(chans), whole(wz.shape), whole(wo.shape),
            whole(skip_row.shape), whole(gain_row.shape),
        ],
        [
            moved(chans), moved(chans),
            pl.BlockSpec((BLOCK, width), lambda i, where: (jnp.minimum(i, 1), 0)),
            pl.BlockSpec((BLOCK, width), lambda i, where: (jnp.maximum(i - 2, 0), 0)),
            pl.BlockSpec((BLOCK, 128), lambda i, where: (i, 0)),
        ],
        [
            out((toks, chans), BF), out((toks, chans), BF), out((toks // 2, width), BF),
            out((toks // 2, width), F32), out((toks, 128), F32),
        ],
        prefetch=1, flops=4 * toks * width * chans, nbytes=14 * toks * chans,
    )(place, n_full, y, xc, wz, wo, skip_row, gain_row)


def loss_kernel(
    near_ref, got_ref, sq_ref, sqgot_ref, res_ref, teach_ref, valid_ref, scale_ref,
    mixed_ref, gres_ref, gs_ref, q_ref, loss_ref, *, inner,
):
    @pl.when(pl.program_id(0) == 0)
    def _():
        loss_ref[...] = jnp.zeros_like(loss_ref)

    total = sq_ref[:, 0:1] + sqgot_ref[:, 0:1]
    factor = lax.rsqrt(total / inner + EPSILON)
    branch = near_ref[...] + got_ref[...].astype(F32)
    result = res_ref[...].astype(F32) + factor * branch
    mixed_ref[...] = result.astype(BF)
    error = result - teach_ref[...].astype(F32)
    valid = valid_ref[...]
    terms = jnp.sum((valid * error * error).reshape(-1, 8, error.shape[1]), axis=0)
    for col in range(0, error.shape[1], 128):
        loss_ref[...] += terms[:, col : col + 128]
    grad = (valid * scale_ref[0:1, 0:1]) * error
    gres_ref[...] = grad
    gs = (grad * factor).astype(BF)
    gs_ref[...] = gs
    prods = jnp.sum(gs.astype(F32) * branch, axis=1, keepdims=True)
    q_ref[...] = jnp.broadcast_to(prods * factor * factor / inner, q_ref.shape)


def loss_step(near, got, sq, sqgot, residual, teacher, valid_col, scale, inner):
    toks, width = near.shape
    nb = toks // BLOCK
    return call(
        functools.partial(loss_kernel, inner=inner),
        (nb,),
        [
            rows(BLOCK, width), rows(BLOCK, width), rows(BLOCK, 128), rows(BLOCK, 128),
            rows(BLOCK, width), rows(BLOCK, width), rows(BLOCK, 1), whole(scale.shape),
        ],
        [
            rows(BLOCK, width), rows(BLOCK, width), rows(BLOCK, width), rows(BLOCK, 128),
            whole((8, 128)),
        ],
        [
            out((toks, width), BF), out((toks, width), F32), out((toks, width), BF),
            out((toks, 128), F32), out((8, 128), F32),
        ],
        nbytes=20 * toks * width,
    )(near, got, sq, sqgot, residual, teacher, valid_col, scale)


def gate_back_kernel(
    gs_ref, q_ref, wo_ref, y_ref, xc_ref, gate_ref, ag_ref, c_ref, skip_ref, gain_ref, spread_ref,
    dz_ref, dy_ref, rowdot_ref, dstart_ref, dgain_ref, dskip_ref, dyf,
):
    @pl.when(pl.program_id(0) == 0)
    def _():
        dstart_ref[...] = jnp.zeros_like(dstart_ref)
        dgain_ref[...] = jnp.zeros_like(dgain_ref)
        dskip_ref[...] = jnp.zeros_like(dskip_ref)

    chans = y_ref.shape[1]
    n_state = c_ref.shape[1]
    q_now = q_ref[:, 0:1]
    gs = gs_ref[...]
    for col in range(0, chans, 256):
        cols = slice(col, col + 256)
        grad = dot_nn(gs, wo_ref[:, cols])
        gate = gate_ref[:, cols].astype(F32)
        sig = sigmoid(gate)
        silu = gate * sig
        x_now = xc_ref[:, cols].astype(F32)
        y_now = y_ref[:, cols]
        mixed = y_now + skip_ref[:, cols] * x_now
        gated = mixed * silu
        dgain_ref[:, cols] += jnp.sum((grad * gated).reshape(-1, 8, 256), axis=0)
        dgated = grad * gain_ref[:, cols] - gated * q_now
        dz_ref[:, cols] = (dgated * mixed * (sig * (1.0 + gate * (1.0 - sig)))).astype(BF)
        dy = (dgated * silu).astype(BF)
        dy_ref[:, cols] = dy
        dy32 = dy.astype(F32)
        dskip_ref[:, cols] += jnp.sum((dy32 * x_now).reshape(-1, 8, 256), axis=0)
        dyf[:, cols] = dy32 * y_now
    spread = spread_ref[...]
    rowdot_ref[...] = per_head(dyf[...], spread)
    scaled = (dy_ref[...].astype(F32) * by_expansion(jnp.exp(ag_ref[...]), spread)).astype(BF)
    dstart_ref[...] += dot_tn(c_ref[...], scaled)


def gate_backward(gs, q, wo, y, xc, gate, ag, bcc, skip_row, gain_row, spread):
    toks, width = gs.shape
    chans = wo.shape[1]
    n_state = bcc.shape[1] // 2
    nb = toks // BLOCK
    return call(
        gate_back_kernel,
        (nb,),
        [
            rows(BLOCK, width), rows(BLOCK, 128), whole(wo.shape), rows(BLOCK, chans),
            rows(BLOCK, chans), rows(BLOCK, chans), rows(BLOCK, HEADS_PAD),
            pl.BlockSpec((BLOCK, n_state), lambda i: (i, 1)), whole(skip_row.shape),
            whole(gain_row.shape), whole(spread.shape),
        ],
        [
            rows(BLOCK, chans), rows(BLOCK, chans), rows(BLOCK, HEADS_PAD),
            whole((n_state, chans)), whole((8, chans)), whole((8, chans)),
        ],
        [
            out((toks, chans), BF), out((toks, chans), BF), out((toks, HEADS_PAD), F32),
            out((n_state, chans), F32), out((8, chans), F32), out((8, chans), F32),
        ],
        [pltpu.VMEM((BLOCK, chans), F32)],
        flops=2 * toks * width * chans, nbytes=14 * toks * chans,
    )(gs, q, wo, y, xc, gate, ag, bcc, skip_row, gain_row, spread)


def scan_back_kernel(
    xc_ref, bcc_ref, dt_ref, a_ref, at_ref, sig_ref, dy_ref, rowdot_ref, saved_ref, xin_ref,
    bcin_ref, dend_ref, cx_ref, cbc_ref, skip_ref, rate_ref, spread_ref,
    dxin_ref, dbc_ref, ddt_ref, dxh_ref, dbch_ref, dcx_ref, dcbc_ref, dhead_ref,
    xt, dstate, dxt, xs, bs, dxp, dbp, dbco,
):
    step = pl.program_id(0)
    block, chans = xc_ref.shape
    bcw = bcc_ref.shape[1]
    n_state = bcw // 2
    half = block // 2
    toks = bcin_ref.shape[0] - HALO

    @pl.when(step == 0)
    def _():
        dstate[...] = dend_ref[...].astype(F32)
        dxp[block : block + 8, :] = jnp.zeros((8, chans), F32)
        dbp[block : block + 8, :] = jnp.zeros((8, bcw), F32)
        dcx_ref[...] = jnp.zeros_like(dcx_ref)
        dcbc_ref[...] = jnp.zeros_like(dcbc_ref)
        dhead_ref[...] = jnp.zeros_like(dhead_ref)

    @pl.when(step > 0)
    def _():
        dxp[block : block + 8, :] = dxp[0:8, :]
        dbp[block : block + 8, :] = dbp[0:8, :]

    spread = spread_ref[...]
    b_now = bcc_ref[:, 0:n_state]
    c_now = bcc_ref[:, n_state:]
    a_now = a_ref[...]
    dt_now = dt_ref[...]
    a_last = a_now[block - 1 : block]
    dt_wide = by_expansion(dt_now, spread)
    xt[...] = (xc_ref[...].astype(F32) * dt_wide).astype(BF)
    tail = by_expansion(jnp.exp(a_last - a_now), spread)
    dstate_low = dstate[...].astype(BF)
    dxt[...] = dot_nn(b_now, dstate_low) * tail
    scores = dot_nt(b_now, c_now)
    row_i = lax.broadcasted_iota(jnp.int32, (half, half), 0)
    col_i = lax.broadcasted_iota(jnp.int32, (half, half), 1)
    shut = jnp.where(row_i <= col_i, 0.0, -1e30).astype(F32)
    lane = lax.broadcasted_iota(jnp.int32, (half, 128), 1)
    lane_full = lax.broadcasted_iota(jnp.int32, (block, 128), 1)
    g_top = jnp.zeros((half, block), F32)
    g_low = jnp.zeros((half, half), F32)
    for pair in range(chans // 128):
        cols = slice(pair * 128, pair * 128 + 128)
        x_pair = xt[:, cols]
        dy_pair = dy_ref[:, cols]
        tops, lows = [], []
        for sub in range(2):
            h = pair * 2 + sub
            mine = (lane_full < HP) if sub == 0 else (lane_full >= HP)
            x_mine = jnp.where(mine, x_pair, jnp.zeros_like(x_pair))
            a_row = at_ref[h : h + 1, :]
            a_top = a_now[0:half, h : h + 1]
            a_low = a_now[half:block, h : h + 1]
            w_top = jnp.exp(a_row[:, 0:half] - a_top + shut)
            w_right = jnp.exp(a_row[:, half:block] - a_top)
            w_low = jnp.exp(a_row[:, half:block] - a_low + shut)
            w_upper = jnp.concatenate([w_top, w_right], axis=1)
            m_upper = (w_upper * scores[0:half]).astype(BF)
            m_low = (w_low * scores[half:block, half:block]).astype(BF)
            tops.append(dot_nn(m_upper, dy_pair))
            lows.append(dot_nn(m_low, dy_pair[half:block]))
            g_top += w_upper * dot_nt(x_mine[0:half], dy_pair)
            g_low += w_low * dot_nt(x_mine[half:block], dy_pair[half:block])
        dxt[0:half, cols] += jnp.where(lane < HP, tops[0], tops[1])
        dxt[half:block, cols] += jnp.where(lane < HP, lows[0], lows[1])
    g_top = g_top.astype(BF)
    g_low = g_low.astype(BF)
    dy_wide = (dy_ref[...].astype(F32) * by_expansion(jnp.exp(a_now), spread)).astype(BF)
    x_tail = (xt[...].astype(F32) * tail).astype(BF)
    d_b = dot_nt(x_tail, dstate_low)
    d_c = dot_nt(dy_wide, saved_ref[0])
    dbco[0:half, 0:n_state] = d_b[0:half] + dot_nn(g_top, c_now)
    dbco[half:block, 0:n_state] = d_b[half:block] + dot_nn(g_low, c_now[half:block])
    d_c_top = dot_tn(g_top, b_now[0:half])
    dbco[0:half, n_state:] = d_c[0:half] + d_c_top[0:half]
    dbco[half:block, n_state:] = (
        d_c[half:block] + d_c_top[half:block] + dot_tn(g_low, b_now[half:block])
    )
    coldot = per_head(dxt[...] * xt[...].astype(F32), spread)
    direct = per_head(dxt[...] * xc_ref[...].astype(F32), spread)
    ends = jnp.sum(dstate[...] * saved_ref[1].astype(F32), axis=0, keepdims=True)
    ends = per_head(jnp.broadcast_to(ends, (8, chans)), spread)
    row_k = lax.broadcasted_iota(jnp.int32, (block, HEADS_PAD), 0)
    d_a = rowdot_ref[...] - coldot + jnp.where(row_k == block - 1, ends[0:1], 0.0)
    row_b = lax.broadcasted_iota(jnp.int32, (block, block), 0)
    col_b = lax.broadcasted_iota(jnp.int32, (block, block), 1)
    onward = jnp.where(row_b <= col_b, 1.0, 0.0).astype(F32)
    d_step = jnp.dot(onward, d_a, precision=HIGH, preferred_element_type=F32)
    rate = rate_ref[0:1, :]
    d_raw = (direct + rate * d_step) * sig_ref[...]
    ddt_ref[...] = d_raw.astype(BF)
    dhead_ref[0:8, :] += jnp.sum(d_raw.reshape(-1, 8, HEADS_PAD), axis=0)
    dhead_ref[8:16, :] += jnp.sum((dt_now * d_step * rate).reshape(-1, 8, HEADS_PAD), axis=0)
    decay = by_expansion(jnp.broadcast_to(jnp.exp(a_last), (8, HEADS_PAD)), spread)
    dstate[...] = dstate[...] * decay[0:1] + dot_tn(c_now, dy_wide)
    first = pl.multiple_of(toks - (step + 1) * block, block)
    last = step == pl.num_programs(0) - 1
    bs[...] = bcin_ref[pl.ds(first, block + HALO), :].astype(F32)
    off = HALO - 3
    for col in range(0, bcw, 128):
        cols = slice(col, col + 128)
        pre = bs[off : off + block, cols] * cbc_ref[0:1, cols]
        for k in range(1, 4):
            pre += bs[off + k : off + k + block, cols] * cbc_ref[k : k + 1, cols]
        sig = sigmoid(pre)
        dpre = dbco[:, cols] * (sig * (1.0 + pre * (1.0 - sig)))
        dbp[0:block, cols] = dpre
        for k in range(4):
            dcbc_ref[8 * k : 8 * k + 8, cols] += jnp.sum(
                (dpre * bs[off + k : off + k + block, cols]).reshape(-1, 8, 128), axis=0
            )
        back = dbp[3 : 3 + block, cols] * cbc_ref[0:1, cols]
        for k in range(1, 4):
            back += dbp[3 - k : 3 - k + block, cols] * cbc_ref[k : k + 1, cols]
        dbc_ref[:, cols] = back.astype(BF)
    for col in range(0, chans, 128):
        cols = slice(col, col + 128)
        xs[...] = xin_ref[pl.ds(first, block + HALO), cols].astype(F32)
        pre = xs[off : off + block] * cx_ref[0:1, cols]
        for k in range(1, 4):
            pre += xs[off + k : off + k + block] * cx_ref[k : k + 1, cols]
        sig = sigmoid(pre)
        grad = dxt[:, cols] * dt_wide[:, cols] + skip_ref[:, cols] * dy_ref[:, cols].astype(F32)
        dpre = grad * (sig * (1.0 + pre * (1.0 - sig)))
        dxp[0:block, cols] = dpre
        for k in range(4):
            dcx_ref[8 * k : 8 * k + 8, cols] += jnp.sum(
                (dpre * xs[off + k : off + k + block]).reshape(-1, 8, 128), axis=0
            )
        back = dxp[3 : 3 + block, cols] * cx_ref[0:1, cols]
        for k in range(1, 4):
            back += dxp[3 - k : 3 - k + block, cols] * cx_ref[k : k + 1, cols]
        dxin_ref[:, cols] = back.astype(BF)

    @pl.when(last)
    def _():
        row_h = lax.broadcasted_iota(jnp.int32, (HALO, 1), 0)
        for src, taps, dest in ((dxp, cx_ref, dxh_ref), (dbp, cbc_ref, dbch_ref)):
            head = src[0:8, :]
            acc = jnp.zeros((HALO, src.shape[1]), F32)
            for t in range(3):
                total = taps[0:1, :] * head[t : t + 1]
                for k in range(1, t + 1):
                    total = total + taps[k : k + 1, :] * head[t - k : t - k + 1]
                acc = acc + jnp.where(row_h == HALO - 3 + t, total, 0.0)
            dest[...] = acc.astype(BF)


def scan_backward(
    xc, bcc, dt, a_cols, a_rows, sig, dy, rowdot, saved, xin_ext, bcin_ext, dend, conv_x, conv_bc,
    skip_row, rate_row, spread,
):
    toks, chans = xc.shape
    bcw = bcc.shape[1]
    n_state = bcw // 2
    heads = chans // HP
    nb = toks // BLOCK

    def back(width):
        return pl.BlockSpec((BLOCK, width), lambda i: (nb - 1 - i, 0))

    return call(
        scan_back_kernel,
        (nb,),
        [
            back(chans), back(bcw), back(HEADS_PAD), back(HEADS_PAD),
            pl.BlockSpec((heads, BLOCK), lambda i: (0, nb - 1 - i)), back(HEADS_PAD),
            back(chans), back(HEADS_PAD),
            pl.BlockSpec((2, n_state, chans), lambda i: (nb - 1 - i, 0, 0)),
            whole(xin_ext.shape), whole(bcin_ext.shape), whole(dend.shape),
            whole(conv_x.shape), whole(conv_bc.shape), whole(skip_row.shape),
            whole(rate_row.shape), whole(spread.shape),
        ],
        [
            back(chans), back(bcw), back(HEADS_PAD), whole((HALO, chans)), whole((HALO, bcw)),
            whole((32, chans)), whole((32, bcw)), whole((16, HEADS_PAD)),
        ],
        [
            out((toks, chans), BF), out((toks, bcw), BF), out((toks, HEADS_PAD), BF),
            out((HALO, chans), BF), out((HALO, bcw), BF), out((32, chans), F32),
            out((32, bcw), F32), out((16, HEADS_PAD), F32),
        ],
        [
            pltpu.VMEM((BLOCK, chans), BF), pltpu.VMEM((n_state, chans), F32),
            pltpu.VMEM((BLOCK, chans), F32), pltpu.VMEM((BLOCK + HALO, 128), F32),
            pltpu.VMEM((BLOCK + HALO, bcw), F32), pltpu.VMEM((BLOCK + 8, chans), F32),
            pltpu.VMEM((BLOCK + 8, bcw), F32), pltpu.VMEM((BLOCK, bcw), F32),
        ],
        flops=2 * toks * BLOCK * chans * 4, nbytes=16 * toks * chans,
    )(
        xc, bcc, dt, a_cols, a_rows, sig, dy, rowdot, saved, xin_ext, bcin_ext, dend, conv_x,
        conv_bc, skip_row, rate_row, spread,
    )


def input_grad_kernel(
    where_ref, dz_ref, dx_ref, dbc_ref, ddt_ref, add_ref, wz_ref, wx_ref, wbc_ref, wdt_ref,
    far_ref, near_ref,
):
    step = pl.program_id(0)
    part = dot_nt(dz_ref[...], wz_ref[...])
    part += dot_nt(dx_ref[...], wx_ref[...])
    part += dot_nt(dbc_ref[...], wbc_ref[...])
    part += dot_nn(ddt_ref[...], wdt_ref[...])
    add = jnp.where(step % 2 == 1, add_ref[...].astype(F32), 0.0)
    core = where_ref[3]

    @pl.when(step < 2)
    def _():
        far_ref[...] = part.astype(BF)

        @pl.when(core == 0)
        def _():
            block = part.shape[0]
            far_ref[block - HALO :, :] = (part[block - HALO :] + add).astype(BF)

    @pl.when(step >= 2)
    def _():
        near_ref[...] = part

        @pl.when(core == 1)
        def _():
            block = part.shape[0]
            near_ref[block - HALO :, :] = part[block - HALO :] + add


def input_grad(place, dz, dxin, dbc, ddt, add, wz, wx, wbc, wdt):
    toks, chans = dz.shape
    width = wz.shape[0]
    nb = toks // BLOCK

    def moved(w):
        return pl.BlockSpec(
            (BLOCK, w), lambda i, where: ((((i // 2) + 1 - where[3]) % 2) * 2 + i % 2, 0)
        )

    return call(
        input_grad_kernel,
        (nb,),
        [
            moved(chans), moved(chans), moved(dbc.shape[1]), moved(HEADS_PAD), whole(add.shape),
            whole(wz.shape), whole(wx.shape), whole(wbc.shape), whole(wdt.shape),
        ],
        [
            pl.BlockSpec((BLOCK, width), lambda i, where: (jnp.minimum(i, 1), 0)),
            pl.BlockSpec((BLOCK, width), lambda i, where: (jnp.maximum(i - 2, 0), 0)),
        ],
        [out((toks // 2, width), BF), out((toks // 2, width), F32)],
        prefetch=1, flops=4 * toks * width * chans, nbytes=8 * toks * chans,
    )(place, dz, dxin, dbc, ddt, add, wz, wx, wbc, wdt)


class Moves:
    def __init__(self, n_dp, n_tensor):
        self.n_dp = n_dp
        self.n_all = n_dp * n_tensor
        self.n_tensor = n_tensor
        dp = lax.axis_index("dp")
        tensor = lax.axis_index("tensor")
        self.dp = dp
        self.row = tensor // 2
        self.core = tensor % 2
        self.z = dp // 2
        self.x = dp % 2
        self.place = jnp.stack([self.z, self.x, self.row, self.core]).astype(jnp.int32)

    def swap(self, value, z=0, x=0, y=0, c=0):
        mask = (z * 2 + x) * self.n_tensor + y * 2 + c
        return lax.ppermute(value, AXES, [(i, i ^ mask) for i in range(self.n_all)])

    def up(self, value):
        pairs = [(i, i + 2) for i in range(self.n_all) if i % self.n_tensor < 2]
        return lax.ppermute(value, AXES, pairs)

    def down(self, value):
        pairs = [(i + 2, i) for i in range(self.n_all) if i % self.n_tensor < 2]
        return lax.ppermute(value, AXES, pairs)


def gather_blocks(moves, block):
    others = [moves.swap(block, z=k) for k in (1, 2, 3)]
    first = jnp.stack([block, others[0]])
    second = jnp.stack([others[1], others[2]])
    first = jnp.stack([first, moves.swap(first, x=1)])
    second = jnp.stack([second, moves.swap(second, y=1)])
    return first, moves.swap(first, y=1), second, moves.swap(second, x=1)


def spots(z, x):
    for kx in range(2):
        for kz in range(2):
            slab = (z ^ kz) * 2 + (x ^ kx)
            yield 0, kx, kz, slab, 0
            yield 1, kx, kz, slab, 1
    for ky in range(2):
        for kz in range(2):
            yield 2, ky, kz, (z ^ (2 + kz)) * 2 + x, ky
            yield 3, ky, kz, (z ^ (2 + kz)) * 2 + (x ^ 1), ky


def place_first_kernel(where_ref, p0, p1, p2, p3, wx_ref, wbc_ref, wdt_ref, count_ref, dts, *, slab):
    pieces = (p0, p1, p2, p3)
    cols = p0.shape[-1]
    z, x, y = where_ref[0], where_ref[1], where_ref[2]
    bc_rows = slab // 4
    total = jnp.zeros((8, 128), F32)
    for arr, i, j, dp, ky in spots(z, x):
        piece = pieces[arr]
        row0 = pl.multiple_of(dp * slab, slab)
        wx_ref[pl.ds(row0, slab), ky * cols : ky * cols + cols] = piece[i, j, 0:slab, :]
        bc0 = pl.multiple_of(dp * slab + (y ^ ky) * 2 * bc_rows, bc_rows)
        bc1 = pl.multiple_of(dp * slab + (y ^ ky) * 2 * bc_rows + bc_rows, bc_rows)
        wbc_ref[pl.ds(bc0, bc_rows), :] = piece[i, j, slab : slab + bc_rows, 0 : cols // 2]
        wbc_ref[pl.ds(bc1, bc_rows), :] = piece[i, j, slab : slab + bc_rows, cols // 2 : cols]
        extra = piece[i, j, slab + bc_rows : slab + bc_rows + 16, 0:slab].astype(F32)
        dts[ky * 8 : ky * 8 + 8, pl.ds(row0, slab)] = extra[0:8]
        total = total + extra[8:16]
    wdt_ref[...] = jnp.zeros_like(wdt_ref)
    wdt_ref[0:16, :] = dts[...].astype(BF)
    count_ref[...] = jnp.broadcast_to(jnp.sum(total[0:1], axis=1, keepdims=True), (8, 128))


def place_second_kernel(where_ref, p0, p1, p2, p3, wz_ref, wo_ref, *, slab):
    pieces = (p0, p1, p2, p3)
    cols = p0.shape[-1]
    for arr, i, j, dp, ky in spots(where_ref[0], where_ref[1]):
        row0 = pl.multiple_of(dp * slab, slab)
        piece = pieces[arr]
        wz_ref[pl.ds(row0, slab), ky * cols : ky * cols + cols] = piece[i, j, 0:slab, :]
        wo_ref[pl.ds(row0, slab), ky * cols : ky * cols + cols] = piece[i, j, slab : 2 * slab, :]


def gather_first(moves, w_x, w_bc, w_dt, counts):
    slab, cols = w_x.shape
    n_dp = moves.n_dp
    width = slab * n_dp
    bcw = w_bc.shape[1]
    if n_dp != 8:
        own = lax.all_gather(w_x, "dp", axis=0, tiled=True)
        wx = jnp.concatenate([own, moves.swap(own, y=1)], axis=1)
        wbc = lax.all_gather(w_bc, "dp", axis=0, tiled=True)
        own = lax.all_gather(w_dt, "dp", axis=0, tiled=True).T
        both = jnp.concatenate([own, moves.swap(own, y=1)], axis=0)
        wdt = jnp.zeros((HEADS_PAD, width), BF).at[0 : both.shape[0]].set(both)
        count = lax.psum(jnp.sum(counts), AXES) / 2.0
        return wx, wbc, wdt, jnp.full((8, 128), count, F32)
    bc_rows = slab // 4
    half = lax.dynamic_slice_in_dim(w_bc, moves.row * 2 * bc_rows, 2 * bc_rows, 0)
    extra = jnp.zeros((16, cols), BF)
    extra = extra.at[0:8, 0:slab].set(w_dt.T)
    extra = extra.at[8, 0:4].set(counts.astype(BF))
    block = jnp.concatenate(
        [w_x, jnp.concatenate([half[0:bc_rows], half[bc_rows:]], axis=1), extra], axis=0
    )
    pieces = gather_blocks(moves, block)
    return call(
        functools.partial(place_first_kernel, slab=slab),
        (1,),
        [whole(p.shape) for p in pieces],
        [
            whole((width, 2 * cols)), whole((width, bcw)), whole((HEADS_PAD, width)),
            whole((8, 128)),
        ],
        [
            out((width, 2 * cols), BF), out((width, bcw), BF), out((HEADS_PAD, width), BF),
            out((8, 128), F32),
        ],
        [pltpu.VMEM((16, width), F32)],
        prefetch=1, nbytes=8 * width * cols,
    )(moves.place, *pieces)


def gather_second(moves, w_z, w_out):
    slab, cols = w_z.shape
    n_dp = moves.n_dp
    width = slab * n_dp
    if n_dp != 8:
        both = []
        for weight in (w_z, w_out):
            own = lax.all_gather(weight, "dp", axis=0, tiled=True)
            both.append(jnp.concatenate([own, moves.swap(own, y=1)], axis=1))
        return tuple(both)
    pieces = gather_blocks(moves, jnp.concatenate([w_z, w_out], axis=0))
    return call(
        functools.partial(place_second_kernel, slab=slab),
        (1,),
        [whole(p.shape) for p in pieces],
        [whole((width, 2 * cols)), whole((width, 2 * cols))],
        [out((width, 2 * cols), BF), out((width, 2 * cols), BF)],
        prefetch=1, nbytes=16 * width * cols,
    )(moves.place, *pieces)


def split_rows(result, hold, x, cols, a_own, a_other, b_own, b_other, step, slab, at):
    hold[...] = result
    near = pl.multiple_of(x * slab, slab)
    far = pl.multiple_of((1 - x) * slab, slab)
    rows_at = slice(at, at + slab)

    @pl.when(step < 2)
    def _():
        a_own[0, 0, rows_at, :] = hold[pl.ds(near, slab), 0:cols].astype(BF)
        a_own[0, 1, rows_at, :] = hold[pl.ds(far, slab), 0:cols].astype(BF)
        a_other[0, 0, rows_at, :] = hold[pl.ds(near, slab), cols:].astype(BF)
        a_other[0, 1, rows_at, :] = hold[pl.ds(far, slab), cols:].astype(BF)

    @pl.when(step >= 2)
    def _():
        b_own[0, 0, rows_at, :] = hold[pl.ds(near, slab), 0:cols].astype(BF)
        b_own[0, 1, rows_at, :] = hold[pl.ds(near, slab), cols:].astype(BF)
        b_other[0, 0, rows_at, :] = hold[pl.ds(far, slab), 0:cols].astype(BF)
        b_other[0, 1, rows_at, :] = hold[pl.ds(far, slab), cols:].astype(BF)


def row_sums(weight, grad):
    ones = jnp.ones((8, weight.shape[1]), BF)
    high, rest = split_low(weight.astype(F32) * grad)
    return (dot_nt(ones, high) + dot_nt(ones, rest))[0:1]


def two_grads_kernel(
    where_ref, n_ref, dz_ref, gs_ref, u_ref, wz_ref, a_own, a_other, b_own, b_other, gain_ref, hold,
    *, slab,
):
    step = pl.program_id(0)
    cols = a_own.shape[-1]
    x = where_ref[1]
    slab_z = where_ref[0] ^ step
    outs = (a_own, a_other, b_own, b_other)
    grad = dot_tn(n_ref[...], dz_ref[...])
    gain_ref[pl.ds(slab_z, 1), :] = row_sums(wz_ref[...], grad)
    split_rows(grad, hold, x, cols, *outs, step, slab, 0)
    split_rows(dot_tn(gs_ref[...], u_ref[...]), hold, x, cols, *outs, step, slab, slab)


def quad_specs(slab_rows, cols):
    first = pl.BlockSpec((1, 2, slab_rows, cols), lambda i, where: (jnp.minimum(i, 1), 0, 0, 0))
    second = pl.BlockSpec((1, 2, slab_rows, cols), lambda i, where: (jnp.maximum(i - 2, 0), 0, 0, 0))
    return [first, first, second, second], [out((2, 2, slab_rows, cols), BF)] * 4


def two_grads(moves, n_full, dz, gs, u, wz):
    toks, width = n_full.shape
    chans = dz.shape[1]
    cols = chans // 2
    slab = width // 8
    specs, shapes = quad_specs(2 * slab, cols)
    lane_block = pl.BlockSpec((toks, 2 * slab), lambda i, where: (0, where[0] ^ i))
    return call(
        functools.partial(two_grads_kernel, slab=slab),
        (4,),
        [
            lane_block, whole(dz.shape), lane_block, whole(u.shape),
            pl.BlockSpec((2 * slab, chans), lambda i, where: (where[0] ^ i, 0)),
        ],
        specs + [whole((4, 2 * slab))],
        shapes + [out((4, 2 * slab), F32)],
        [pltpu.VMEM((2 * slab, chans), F32)],
        prefetch=1, flops=4 * toks * width * chans, nbytes=16 * toks * chans,
    )(moves.place, n_full, dz, gs, u, wz)


def last_grads_kernel(
    where_ref, n_ref, halo_ref, dx_ref, dxh_ref, dbc_ref, dbch_ref, ddt_ref, wx_ref, wbc_ref,
    wdt_ref, a_own, a_other, b_own, b_other, gain_ref, dwdt_ref, hold, hold_bc, *, slab,
):
    step = pl.program_id(0)
    cols = a_own.shape[-1]
    z, x, y, core = where_ref[0], where_ref[1], where_ref[2], where_ref[3]
    slab_z = z ^ step
    n_now = n_ref[...]
    grad = dot_tn(n_now, dx_ref[...]) + dot_tn(halo_ref[...], dxh_ref[...])
    grad_bc = dot_tn(n_now, dbc_ref[...]) + dot_tn(halo_ref[...], dbch_ref[...])
    grad_dt = dot_tn(ddt_ref[...], n_now)
    dwdt_ref[...] = grad_dt[0:16]
    sums = row_sums(wx_ref[...], grad) + 0.5 * row_sums(wbc_ref[...], grad_bc)
    sums += jnp.sum(grad_dt * wdt_ref[...].astype(F32), axis=0, keepdims=True)
    gain_ref[pl.ds(slab_z, 1), :] = sums
    split_rows(grad, hold, x, cols, a_own, a_other, b_own, b_other, step, slab, 0)
    hold_bc[...] = grad_bc
    quarter = slab // 4
    eighth = quarter // 2
    rows_at = slice(slab, slab + eighth)

    def bc_block(kx, ky):
        start = pl.multiple_of((x ^ kx) * slab + ((y ^ ky) * 2 + core) * quarter, quarter)
        block = hold_bc[pl.ds(start, quarter), :].astype(BF)
        return jnp.concatenate([block[0:eighth], block[eighth:]], axis=1)

    @pl.when(step < 2)
    def _():
        a_own[0, 0, rows_at, :] = bc_block(0, 0)
        a_own[0, 1, rows_at, :] = bc_block(1, 0)
        a_other[0, 0, rows_at, :] = bc_block(0, 1)
        a_other[0, 1, rows_at, :] = bc_block(1, 1)

    @pl.when(step >= 2)
    def _():
        b_own[0, 0, rows_at, :] = bc_block(0, 0)
        b_own[0, 1, rows_at, :] = bc_block(0, 1)
        b_other[0, 0, rows_at, :] = bc_block(1, 0)
        b_other[0, 1, rows_at, :] = bc_block(1, 1)


def last_grads(moves, n_full, halo, dxin, dxh, dbc, dbch, ddt, wx, wbc, wdt):
    toks, width = n_full.shape
    chans = dxin.shape[1]
    bcw = dbc.shape[1]
    cols = chans // 2
    slab = width // 8
    specs, shapes = quad_specs(slab + slab // 8, cols)
    lane_block = pl.BlockSpec((toks, 2 * slab), lambda i, where: (0, where[0] ^ i))
    return call(
        functools.partial(last_grads_kernel, slab=slab),
        (4,),
        [
            lane_block, pl.BlockSpec((HALO, 2 * slab), lambda i, where: (0, where[0] ^ i)),
            whole(dxin.shape), whole(dxh.shape), whole(dbc.shape), whole(dbch.shape),
            whole(ddt.shape), pl.BlockSpec((2 * slab, chans), lambda i, where: (where[0] ^ i, 0)),
            pl.BlockSpec((2 * slab, bcw), lambda i, where: (where[0] ^ i, 0)),
            pl.BlockSpec((HEADS_PAD, 2 * slab), lambda i, where: (0, where[0] ^ i)),
        ],
        specs + [
            whole((4, 2 * slab)), pl.BlockSpec((16, 2 * slab), lambda i, where: (0, where[0] ^ i)),
        ],
        shapes + [out((4, 2 * slab), F32), out((16, width), F32)],
        [pltpu.VMEM((2 * slab, chans), F32), pltpu.VMEM((2 * slab, bcw), F32)],
        prefetch=1, flops=2 * toks * width * chans, nbytes=16 * toks * chans,
    )(moves.place, n_full, halo, dxin, dxh, dbc, dbch, ddt, wx, wbc, wdt)


def add_low(first, second):
    return (first.astype(F32) + second.astype(F32)).astype(BF)


def reduce_blocks(moves, a_own, a_other, b_own, b_other, ride=None):
    if ride is None:
        a_sum = add_low(a_own, moves.swap(a_other, y=1))
    else:
        shape = a_other.shape
        sent = jnp.concatenate([a_other.reshape(-1, shape[-1]), ride], axis=0)
        n_main = sent.shape[0] - ride.shape[0]
        got = moves.swap(sent, y=1)
        a_sum = add_low(a_own, got[:n_main].reshape(shape))
        ride = add_pair(ride, got[n_main:])
    b_sum = add_low(b_own, moves.swap(b_other, x=1))
    if ride is None:
        a_sum = add_low(a_sum[:, 0], moves.swap(a_sum[:, 1], x=1))
    else:
        shape = a_sum[:, 1].shape
        sent = jnp.concatenate([a_sum[:, 1].reshape(-1, shape[-1]), ride], axis=0)
        got = moves.swap(sent, x=1)
        a_sum = add_low(a_sum[:, 0], got[:n_main // 2].reshape(shape))
        ride = add_pair(ride, got[n_main // 2 :])
    b_sum = add_low(b_sum[:, 0], moves.swap(b_sum[:, 1], y=1))
    total = a_sum[0].astype(F32)
    sends = (a_sum[1], b_sum[0], b_sum[1])
    if ride is None:
        for k, sent in enumerate(sends):
            total = total + moves.swap(sent, z=k + 1).astype(F32)
        return total, None
    n_main = total.shape[0]
    rides = join_pair(ride)
    for k, sent in enumerate(sends):
        got = moves.swap(jnp.concatenate([sent, ride], axis=0), z=k + 1)
        total = total + got[:n_main].astype(F32)
        rides = rides + join_pair(got[n_main:])
    return total, rides


def make_pair(values):
    high, rest = split_low(values)
    return jnp.concatenate([high, rest], axis=0)


def join_pair(pair):
    n = pair.shape[0] // 2
    return pair[:n].astype(F32) + pair[n:].astype(F32)


def add_pair(first, second):
    return make_pair(join_pair(first) + join_pair(second))


def body(
    residual, teacher, valid_mask, gain_in, w_z, w_x, w_bc, w_dt, conv_x, conv_bc, dt_bias, a_log,
    d_skip, gain_gate, w_out,
):
    _, pos_dev, width = residual.shape
    n_tensor = lax.axis_size("tensor")
    n_dp = lax.axis_size("dp")
    moves = Moves(n_dp, n_tensor)
    tokens_all = pos_dev * n_tensor * n_dp
    cols = w_z.shape[1]
    chans = 2 * cols
    own_heads = w_dt.shape[1]
    heads = 2 * own_heads
    inner = cols * n_tensor
    bcw = w_bc.shape[1]
    slab = w_z.shape[0]
    toks = 2 * pos_dev
    core = moves.core

    valid = valid_mask.reshape(pos_dev).astype(F32)
    counts = jnp.sum(valid.reshape(2, pos_dev // 2), axis=1)
    counts = jnp.concatenate([counts, moves.swap(counts, c=1)])

    pack = jnp.concatenate(
        [
            conv_x, gain_gate[None],
            jnp.concatenate(
                [dt_bias, a_log, d_skip, jnp.zeros((cols - 3 * own_heads,), F32)]
            )[None],
            jnp.zeros((2, cols), F32),
        ],
        axis=0,
    )
    pack_other = moves.swap(pack, y=1)
    conv_x_core = jnp.concatenate([pack[0:4], pack_other[0:4]], axis=1)
    gain_row = jnp.concatenate([pack[4:5], pack_other[4:5]], axis=1)

    def head_param(k):
        at = slice(k * own_heads, (k + 1) * own_heads)
        return jnp.concatenate([pack[5, at], pack_other[5, at]])

    def pad_heads(values):
        return jnp.concatenate([values, jnp.zeros((HEADS_PAD - heads,), F32)])

    bias_col = pad_heads(head_param(0))[:, None]
    rates = pad_heads(-jnp.exp(head_param(1)))
    rate_col = rates[:, None]
    rate_row = rates[None, :]
    skip_row = jnp.repeat(head_param(2), HP)[None]
    spread = (
        jnp.arange(HEADS_PAD)[:, None] == (jnp.arange(chans) // HP)[None, :]
    ).astype(BF)

    upper = residual.reshape(pos_dev, width).astype(F32)
    factor = lax.rsqrt(jnp.mean(upper * upper, axis=-1, keepdims=True) + EPSILON)
    normed = (upper * factor * gain_in).astype(BF)
    normed_other = moves.swap(normed, c=1)
    n_full = jnp.where(
        core == 0,
        jnp.concatenate([normed, normed_other], axis=0),
        jnp.concatenate([normed_other, normed], axis=0),
    )
    halo = moves.up(n_full[toks - HALO :])

    wx, wbc, wdt, count_tile = gather_first(moves, w_x, w_bc, w_dt, counts)
    wz, wo = gather_second(moves, w_z, w_out)
    scale = tokens_all / count_tile

    (
        xin, xc, bcin, bcc, dt, a_cols, a_glob, sig, a_rows, state_end,
    ) = front(n_full, halo, wx, wbc, wdt, conv_x_core, conv_bc, bias_col, rate_col, spread)

    def cross(values):
        return jnp.concatenate([values[:, cols:], values[:, :cols]], axis=1)

    state_start = cross(moves.up(state_end.astype(BF)))
    y, saved = scan_forward(xc, bcc, dt, a_cols, a_rows, state_start, spread)
    gate, u, far, near, squares = gate_out_proj(
        moves.place, n_full, y, xc, wz, wo, skip_row, gain_row
    )
    got = moves.swap(far, c=1)
    sq_got = moves.swap(squares[0:pos_dev], c=1)
    mixed, grad_result, gs, q, loss_part = loss_step(
        near, got, squares[pos_dev:], sq_got, residual.reshape(pos_dev, width),
        teacher.reshape(pos_dev, width), valid[:, None], scale, inner,
    )

    def both(mine):
        other = moves.swap(mine, c=1)
        return jnp.where(
            core == 0,
            jnp.concatenate([mine, other], axis=0),
            jnp.concatenate([other, mine], axis=0),
        )

    gs_full = both(gs)
    q_full = both(q)
    dz, dy, rowdot, dstart, dgain_gate, dskip = gate_backward(
        gs_full, q_full, wo, y, xc, gate, a_glob, bcc, skip_row, gain_row, spread
    )
    dend = cross(moves.down(dstart.astype(BF)))

    if n_dp == 8:
        a_own, a_other, b_own, b_other, gain_z = two_grads(moves, n_full, dz, gs_full, u, wz)
        zo_grad, _ = reduce_blocks(moves, a_own, a_other, b_own, b_other)
        grad_w_z, grad_w_out = zo_grad[:slab], zo_grad[slab:]
    else:
        grad_z = dot_tn(n_full, dz)
        grad_o = dot_tn(gs_full, u)

    xin_halo = dot_nn(halo, wx).astype(BF)
    bcin_halo = dot_nn(halo, wbc).astype(BF)
    (
        dxin, dbc, ddt, dxh, dbch, dconv_x, dconv_bc, dhead,
    ) = scan_backward(
        xc, bcc, dt, a_cols, a_rows, sig, dy, rowdot, saved,
        jnp.concatenate([xin_halo, xin], axis=0), jnp.concatenate([bcin_halo, bcin], axis=0),
        dend, conv_x_core, conv_bc, skip_row, rate_row, spread,
    )

    halo_grad = moves.down((dot_nt(dxh, wx) + dot_nt(dbch, wbc)).astype(BF))
    far, near = input_grad(moves.place, dz, dxin, dbc, ddt, halo_grad, wz, wx, wbc, wdt)
    grad_normed = near + moves.swap(far, c=1).astype(F32)

    def in_order(values):
        half = values.shape[-1] // 2
        turned = jnp.concatenate([values[..., half:], values[..., :half]], axis=-1)
        return jnp.where(moves.row == 0, values, turned)

    def head_sum(at):
        return in_order(dhead[at : at + 8, 0:heads].sum(axis=0))

    small = [
        in_order(dconv_x.reshape(4, 8, chans).sum(axis=1)),
        in_order(dgain_gate.sum(axis=0)),
        head_sum(0),
        head_sum(8),
        in_order(dskip.sum(axis=0).reshape(heads, HP).sum(axis=1)),
    ]
    shared = [dconv_bc.reshape(4, 8, bcw).sum(axis=1), loss_part.sum()]
    if n_dp == 8:
        dbc_sum = add_low(dbc, moves.swap(dbc, c=1))
        dbch_sum = add_low(dbch, moves.swap(dbch, c=1))
        a_own, a_other, b_own, b_other, gain_x, grad_dt = last_grads(
            moves, n_full, halo, dxin, dxh, dbc_sum, dbch_sum, ddt, wx, wbc, wdt
        )
        shared.append((gain_z + gain_x).reshape(-1) / gain_in)
        small.append(in_order(grad_dt.T))
        flat = jnp.concatenate([v.reshape(-1) for v in small + shared])
        n_flat = flat.shape[0]
        per_row = cols * 16
        n_pad = -(-n_flat // per_row) * per_row
        ride = make_pair(
            jnp.concatenate([flat, jnp.zeros((n_pad - n_flat,), F32)]).reshape(-1, cols)
        )
        x_grad, sums = reduce_blocks(moves, a_own, a_other, b_own, b_other, ride)
        sums = sums.reshape(-1)
        grad_w_x = x_grad[:slab]
        bc_own = x_grad[slab:]
        bc_own = jnp.concatenate([bc_own[:, :bcw], bc_own[:, bcw:]], axis=0)
        bc_c = moves.swap(bc_own, c=1)
        bc_two = jnp.where(
            core == 0,
            jnp.concatenate([bc_own, bc_c], axis=0),
            jnp.concatenate([bc_c, bc_own], axis=0),
        )
        bc_y = moves.swap(bc_two, y=1)
        grad_w_bc = jnp.where(
            moves.row == 0,
            jnp.concatenate([bc_two, bc_y], axis=0),
            jnp.concatenate([bc_y, bc_two], axis=0),
        )
    else:
        grad_x = dot_tn(n_full, dxin) + dot_tn(halo, dxh)
        grad_bc = dot_tn(n_full, dbc) + dot_tn(halo, dbch)
        grad_dt = dot_tn(ddt, n_full)[0:heads]
        gain_sum = jnp.sum(wz.astype(F32) * grad_z, axis=1)
        gain_sum += jnp.sum(wx.astype(F32) * grad_x, axis=1)
        gain_sum += jnp.sum(wbc.astype(F32) * grad_bc, axis=1)
        gain_sum += jnp.sum(wdt[0:heads].astype(F32) * grad_dt, axis=0)
        shared.append(gain_sum / gain_in)
        small.append(in_order(grad_dt.T))
        big = jnp.stack([grad_z, grad_o, grad_x])
        big = big[:, :, :cols] + moves.swap(big[:, :, cols:], y=1)
        big = lax.psum_scatter(big, "dp", scatter_dimension=1, tiled=True)
        grad_w_z, grad_w_out, grad_w_x = big[0], big[1], big[2]
        grad_w_bc = lax.psum_scatter(
            lax.psum(grad_bc, "tensor"), "dp", scatter_dimension=0, tiled=True
        )
        sums = lax.psum(jnp.concatenate([v.reshape(-1) for v in small + shared]), "dp")
        sums = sums + moves.swap(sums, y=1)
    done = []
    at = 0
    for value in small + shared:
        done.append(sums[at : at + value.size].reshape(value.shape))
        at += value.size
    n_small = len(small)
    first_shared = sum(v.size for v in small)
    tail = sums[first_shared:at]
    tail = tail + moves.swap(tail, c=1)
    n_conv = 4 * bcw
    grad_conv_bc = tail[:n_conv].reshape(4, bcw)
    loss = tail[n_conv] / (count_tile[0, 0] * width)
    grad_gain_in = tail[n_conv + 1 :]

    def own(value):
        half = value.shape[-1] // 2
        return lax.dynamic_slice_in_dim(value, moves.row * half, half, value.ndim - 1)

    g_conv_x, g_gain_gate, g_bias, g_log, g_skip, g_dt = [own(v) for v in done[:n_small]]
    g_dt = lax.dynamic_slice_in_dim(g_dt, moves.dp * slab, slab, 0)

    hat = upper * factor
    scaled = grad_normed * gain_in
    grad_upper = factor * (scaled - hat * jnp.mean(scaled * hat, axis=-1, keepdims=True))
    grad_residual = (grad_result + grad_upper).astype(BF)
    return (
        mixed[None], loss, grad_residual[None], grad_gain_in, grad_w_z, grad_w_x, grad_w_bc, g_dt,
        g_conv_x, grad_conv_bc, g_bias, g_log, g_skip, g_gain_gate, grad_w_out,
    )


def solution(mesh):
    both = P("dp", "tensor")
    tokens = P("dp", "tensor", None)
    return jax.shard_map(
        body,
        mesh=mesh,
        in_specs=(
            tokens, tokens, both, P(), both, both, P("dp", None), both, P(None, "tensor"), P(),
            P("tensor"), P("tensor"), P("tensor"), P("tensor"), both,
        ),
        out_specs=(
            tokens, P(), tokens, P(), both, both, P("dp", None), both, P(None, "tensor"), P(),
            P("tensor"), P("tensor"), P("tensor"), P("tensor"), both,
        ),
        check_vma=False,
    )
```

time: 1150 us -> 379 us (0.33)
  waiting for transfers between devices: 411 us -> 107 us
  matrix products: 280 us -> 2.89 us
  blocking collectives: 150 us -> 0 us
  Pallas kernels: 0 us -> 133 us
  other arithmetic: 154 us -> 38.3 us
  local copies, waits for them, and re-layouts: 126 us -> 27.9 us
  starting transfers between devices: 0.49 us -> 61.4 us
  between operations: 18.4 us -> 3.96 us
    reduce_scatter x6 -> x0, waiting for transfers between devices: 321 us -> none  [the longest x1 71.7 us: body(): lax.psum_scatter(back_rows.reshape(n_seqs, length, width), 'tensor', scat...]
    dot_general x127 -> x4, matrix products: 280 us -> 2.89 us  [the longest x2 2.33 us: dot_nt(): lax.dot_general(left, right, (((1,), (1,)), ((), ())), preferred_element_...]
    pallas_call x0 -> x11, Pallas kernels: none -> 133 us  [the longest x1 31.1 us: scan_backward(): call(scan_back_kernel, (nb,), [back(chans), back(bcw), back(HEADS_PAD), b...]
    ppermute x0 -> x45, waiting for transfers between devices: none -> 107 us  [the longest x41 83.9 us: swap(): return lax.ppermute(value, AXES, [(i, i ^ mask) for i in range(self.n_all)])]
    psum x4 -> x0, blocking collectives: 91.4 us -> none  [the longest x1 40.6 us: body(): lax.psum((loss_part, grad_gain_part, spread_out(grad_conv_x, tensor_pos,...]
    ppermute x0 -> x45, starting transfers between devices: none -> 61.4 us  [the longest x41 51.4 us: swap(): return lax.ppermute(value, AXES, [(i, i ^ mask) for i in range(self.n_all)])]
    all_gather x2 -> x0, blocking collectives: 59.1 us -> none  [the longest x1 31.3 us: body(): lax.all_gather(w_bc, 'dp', axis=0, tiled=True)]
    another operation x96 -> x10, other arithmetic: 50.6 us -> 2.97 us  [the longest x4 1.2 us: gather_blocks(): first = jnp.stack([first, moves.swap(first, x=1)])]
  transfers between devices with their start and end apart: 12 -> 45, of which waited for: 9 -> 15; matrix products, arithmetic and copies ran while one was open for 23% -> 14% of each run, Pallas kernels for 0% -> 26%
where the time goes in v1:
time: 379 us; the launch traced here: 375 us
  Pallas kernels  133 us (35%)
  waiting for transfers between devices  107 us (28%)
  starting transfers between devices  61.4 us (16%)
  other arithmetic  38.3 us (10%)
  local copies, waits for them, and re-layouts  27.9 us (7%)
  between operations  3.96 us (1%)
    ppermute x41, waiting for transfers between devices, swap(): return lax.ppermute(value, AXES, [(i, i ^ mask) for i in range(self.n_all)])  83.9 us
    ppermute x41, starting transfers between devices, swap(): return lax.ppermute(value, AXES, [(i, i ^ mask) for i in range(self.n_all)])  51.4 us
    pallas_call x1, Pallas kernels, scan_backward(): call(scan_back_kernel, (nb,), [back(chans), back(bcw), back(HEADS_PAD), b...  31.1 us
    ppermute x2, waiting for transfers between devices, up(): return lax.ppermute(value, AXES, pairs)  19.8 us
    pallas_call x1, Pallas kernels, two_grads(): call(functools.partial(two_grads_kernel, slab=slab), (4,), [lane_block, w...  14.6 us
    pallas_call x1, Pallas kernels, front(): call(front_kernel, (nb,), [rows(BLOCK, width), whole(halo.shape), whole(w...  14.6 us
    pallas_call x1, Pallas kernels, gate_out_proj(): call(gate_kernel, (nb,), [moved(width), moved(chans), moved(chans), whole...  12.9 us
    pallas_call x1, Pallas kernels, gate_backward(): call(gate_back_kernel, (nb,), [rows(BLOCK, width), rows(BLOCK, 128), whol...  12.5 us
  transfers between devices with their start and end apart: 45, of which 15 were waited for; matrix products, arithmetic and copies ran while one was open for 14% of the time, Pallas kernels for 26%

profile of v1, /device:TPU:0, one launch (start us, length us, event | category | flops | bytes accessed | tf_op | source)
XLA Modules:
  0.0 375.1 jit_solution(3359270236881581653)
XLA Ops:
  2.6 4.1 %collective-permute-start.15 = (bf16[256,512]{1,0:T(8,128)(2,1)S(1)}, bf16[256,512]{1,0:T(8,128)(2,1)S(1)}, u32[]{:S(2)}, u32[]{:S(2)}) collective-permute-start(bf16[256,512]{1,0:T(8,128)(2,1)S(1)} %constant_dynamic-update-slice_fusion), channel_id=1, source_target_pairs={{0,16},{1,17},{2,18},{3,19},{4,20},{5,21},{6,22},{7,23},{8,24},{9,... | collective-permute-start | bytes 786440 | tf_op jit(solution)/shard_map/ppermute | solution.py:706
  20.8 21.6 %collective-permute-done.6 = bf16[176,512]{1,0:T(8,128)(2,1)S(1)} collective-permute-done((bf16[176,512]{1,0:T(8,128)(2,1)S(1)}, bf16[176,512]{1,0:T(8,128)(2,1)S(1)}, u32[]{:S(2)}, u32[]{:S(2)}) %collective-permute-start.6) | collective-permute-done | bytes 180256 | tf_op jit(solution)/shard_map/ppermute | solution.py:706
  60.1 4.8 %collective-permute-done.17 = bf16[2,256,512]{2,1,0:T(8,128)(2,1)S(1)} collective-permute-done((bf16[2,256,512]{2,1,0:T(8,128)(2,1)S(1)}, bf16[2,256,512]{2,1,0:T(8,128)(2,1)S(1)}, u32[]{:S(2)}, u32[]{:S(2)}) %collective-permute-start.17) | collective-permute-done | bytes 524320 | tf_op jit(solution)/shard_map/ppermute | solution.py:706
  75.1 7.4 %collective-permute-done.9.p3 = bf16[2,2,176,512]{3,2,1,0:T(8,128)(2,1)} collective-permute-done((bf16[2,2,176,512]{3,2,1,0:T(8,128)(2,1)}, bf16[2,2,176,512]{3,2,1,0:T(8,128)(2,1)}, u32[]{:S(2)}, u32[]{:S(2)}) %collective-permute-start.9) | collective-permute-done | bytes 720928 | tf_op jit(solution)/shard_map/ppermute | solution.py:706
  82.5 4.2 %shard_map.262 = (bf16[1024,1024]{1,0:T(8,128)(2,1)}, bf16[1024,256]{1,0:T(8,128)(2,1)}, bf16[128,1024]{1,0:T(8,128)(2,1)}, f32[8,128]{1,0:T(8,128)}) custom-call(s32[4]{0:T(128)} %pad_add_fusion.where_ref, bf16[2,2,176,512]{3,2,1,0:T(8,128)(2,1)} %pad_maximum_fusion.3.p0, bf16[2,2,176,512]{3,2,1,0:T(8,128)(2,1)} %collective-permute-done.5.p1, ...), custom_call_target="tpu_custom_call" | custom-call | bytes 4194304 | tf_op jit(solution)/shard_map/pallas_call | solution.py:793
  86.7 15.8 %collective-permute-done.1.halo_ref = bf16[16,1024]{1,0:T(8,128)(2,1)S(1)} collective-permute-done((bf16[16,1024]{1,0:T(8,128)(2,1)S(1)}, bf16[16,1024]{1,0:T(8,128)(2,1)S(1)}, u32[]{:S(2)}, u32[]{:S(2)}) %collective-permute-start.1) | collective-permute-done | bytes 32800 | tf_op jit(solution)/shard_map/ppermute | solution.py:710
  103.1 14.6 %shard_map.263 = (bf16[1024,1024]{1,0:T(8,128)(2,1)}, bf16[1024,1024]{1,0:T(8,128)(2,1)}, bf16[1024,256]{1,0:T(8,128)(2,1)}, bf16[1024,256]{1,0:T(8,128)(2,1)}, ...) custom-call(bf16[1024,1024]{1,0:T(8,128)(2,1)} %copy-done.6, ...), custom_call_target="tpu_custom_call" | custom-call | flops 2684354560 | bytes 8388608 | tf_op jit(solution)/shard_map/pallas_call | solution.py:157
  118.8 4.6 %collective-permute-start.11 = (bf16[128,1024]{1,0:T(8,128)(2,1)S(1)}, bf16[128,1024]{1,0:T(8,128)(2,1)S(1)}, u32[]{:S(2)}, u32[]{:S(2)}) collective-permute-start(bf16[128,1024]{1,0:T(8,128)(2,1)S(1)} %convert_element_type.275), channel_id=1, source_target_pairs={{0,2},{1,3},{4,6},{5,7},{8,10},{9,11},{12,14},{13,15},{16,18},{17,... | collective-permute-start | bytes 786440 | tf_op jit(solution)/shard_map/ppermute | solution.py:710
  124.7 4.0 %collective-permute-done.11 = bf16[128,1024]{1,0:T(8,128)(2,1)S(1)} collective-permute-done((bf16[128,1024]{1,0:T(8,128)(2,1)S(1)}, bf16[128,1024]{1,0:T(8,128)(2,1)S(1)}, u32[]{:S(2)}, u32[]{:S(2)}) %collective-permute-start.11) | collective-permute-done | bytes 262176 | tf_op jit(solution)/shard_map/ppermute | solution.py:710
  129.5 10.6 %shard_map.264 = (f32[1024,1024]{1,0:T(8,128)}, bf16[8,128,1024]{2,1,0:T(8,128)(2,1)}) custom-call(bf16[1024,1024]{1,0:T(8,128)(2,1)} %get-tuple-element.97.xc_ref, bf16[1024,256]{1,0:T(8,128)(2,1)} %get-tuple-element.98.bcc_ref.c_ref, f32[1024,128]{1,0:T(8,128)} %get-tuple-element.99.dt_ref, f32[1024,128]{1,0:T(8,128)} %get-tuple-element.100.a_ref, ...), custom_call_target="tpu_custom_call" | custom-call | flops 1073741824 | bytes 10485760 | tf_op jit(solution)/shard_map/pallas_call | solution.py:243
  140.0 5.2 %shard_map.265 = (bf16[1024,1024]{1,0:T(8,128)(2,1)}, bf16[1024,1024]{1,0:T(8,128)(2,1)}) custom-call(s32[4]{0:T(128)} %pad_add_fusion.where_ref, bf16[2,2,256,512]{3,2,1,0:T(8,128)(2,1)} %copy-done.5, bf16[2,2,256,512]{3,2,1,0:T(8,128)(2,1)} %collective-permute-done.14.p1, bf16[2,2,256,512]{3,2,1,0:T(8,128)(2,1)} %copy-done.4, ...), custom_call_target="tpu_custom_call" | custom-call | bytes 8388608 | tf_op jit(solution)/shard_map/pallas_call | solution.py:821
  145.2 12.9 %shard_map.266 = (bf16[1024,1024]{1,0:T(8,128)(2,1)}, bf16[1024,1024]{1,0:T(8,128)(2,1)}, bf16[512,1024]{1,0:T(8,128)(2,1)}, f32[512,1024]{1,0:T(8,128)}, f32[1024,128]{1,0:T(8,128)}) custom-call(s32[4]{0:T(128)} %pad_add_fusion.where_ref, bf16[1024,1024]{1,0:T(8,128)(2,1)} %copy-done.6, f32[1024,1024]{1,0:T(8,128)} %get-tuple-element.103.y_ref, ...), custom_call_target="tpu_custom_call" | custom-call | flops 4294967296 | bytes 14680064 | tf_op jit(solution)/shard_map/pallas_call | solution.py:299
  162.9 5.2 %shard_map.267 = (bf16[512,1024]{1,0:T(8,128)(2,1)}, f32[512,1024]{1,0:T(8,128)}, bf16[512,1024]{1,0:T(8,128)(2,1)}, f32[512,128]{1,0:T(8,128)}, f32[8,128]{1,0:T(8,128)}) custom-call(f32[512,1024]{1,0:T(8,128)} %get-tuple-element.106.near_ref, bf16[512,1024]{1,0:T(8,128)(2,1)} %copy-done.12, f32[512,128]{1,0:T(8,128)} %get-tuple-element.192.sq_ref, ...), custom_call_target="tpu_custom_call" | custom-call | bytes 10485760 | tf_op jit(solution)/shard_map/pallas_call | solution.py:349
  175.0 4.7 %maximum_select_fusion.1.gs_ref = bf16[1024,1024]{1,0:T(8,128)(2,1)} fusion(bf16[512,1024]{1,0:T(8,128)(2,1)} %collective-permute-done.21, bf16[512,1024]{1,0:T(8,128)(2,1)} %get-tuple-element.112, pred[]{:T(512)S(6)} %eq.49), kind=kLoop, calls=%fused_computation.14 | loop fusion | flops 9437184 | bytes 4194305 | tf_op jit(solution)/shard_map/jit(_where)/select_n | solution.py:1111
  179.7 12.5 %shard_map.268 = (bf16[1024,1024]{1,0:T(8,128)(2,1)}, bf16[1024,1024]{1,0:T(8,128)(2,1)}, f32[1024,128]{1,0:T(8,128)}, f32[128,1024]{1,0:T(8,128)}, f32[8,1024]{1,0:T(8,128)}, /*index=5*/f32[8,1024]{1,0:T(8,128)}) custom-call(bf16[1024,1024]{1,0:T(8,128)(2,1)} %maximum_select_fusion.1.gs_ref, f32[1024,128]{1,0:T(8,128)} %maximum_select_fusion.2.q_ref, ...), custom_call_target="tpu_custom_call" | custom-call | flops 2147483648 | bytes 14680064 | tf_op jit(solution)/shard_map/pallas_call | solution.py:411
  196.6 14.6 %shard_map.271 = (bf16[2,2,256,512]{3,2,1,0:T(8,128)(2,1)}, bf16[2,2,256,512]{3,2,1,0:T(8,128)(2,1)}, bf16[2,2,256,512]{3,2,1,0:T(8,128)(2,1)}, bf16[2,2,256,512]{3,2,1,0:T(8,128)(2,1)}, f32[4,256]{1,0:T(4,128)}) custom-call(s32[4]{0:T(128)} %pad_add_fusion.where_ref, bf16[1024,1024]{1,0:T(8,128)(2,1)} %copy-done.6, ...), custom_call_target="tpu_custom_call" | custom-call | flops 4294967296 | bytes 16777216 | tf_op jit(solution)/shard_map/pallas_call | solution.py:886
  218.6 31.1 %shard_map.269 = (bf16[1024,1024]{1,0:T(8,128)(2,1)}, bf16[1024,256]{1,0:T(8,128)(2,1)}, bf16[1024,128]{1,0:T(8,128)(2,1)}, bf16[16,1024]{1,0:T(8,128)(2,1)}, bf...) custom-call(bf16[1024,1024]{1,0:T(8,128)(2,1)} %get-tuple-element.97.xc_ref, ...), custom_call_target="tpu_custom_call" | custom-call | flops 2147483648 | bytes 16777216 | tf_op jit(solution)/shard_map/pallas_call | solution.py:599
  256.9 3.6 collective-permute-done.34.add_ref
  261.1 11.8 %shard_map.272 = (bf16[512,1024]{1,0:T(8,128)(2,1)}, f32[512,1024]{1,0:T(8,128)}) custom-call(s32[4]{0:T(128)} %pad_add_fusion.where_ref, bf16[1024,1024]{1,0:T(8,128)(2,1)} %get-tuple-element.134.dz_ref, bf16[1024,1024]{1,0:T(8,128)(2,1)} %get-tuple-element.126.dx_ref, bf16[1024,256]{1,0:T(8,128)(2,1)} %get-tuple-element.128.dbc_ref, ...), custom_call_target="tpu_custom_call" | custom-call | flops 4294967296 | bytes 8388608 | tf_op jit(solution)/shard_map/pallas_call | solution.py:674
  273.9 10.7 %shard_map.270 = (bf16[2,2,144,512]{3,2,1,0:T(8,128)(2,1)}, bf16[2,2,144,512]{3,2,1,0:T(8,128)(2,1)}, bf16[2,2,144,512]{3,2,1,0:T(8,128)(2,1)}, bf16[2,2,144,512...) custom-call(s32[4]{0:T(128)} %pad_add_fusion.where_ref, bf16[1024,1024]{1,0:T(8,128)(2,1)} %copy-done.6, ...), custom_call_target="tpu_custom_call" | custom-call | flops 2147483648 | bytes 16777216 | tf_op jit(solution)/shard_map/pallas_call | solution.py:950
  301.3 6.9 %collective-permute-done.26 = bf16[672,512]{1,0:T(8,128)(2,1)S(1)} collective-permute-done((bf16[672,512]{1,0:T(8,128)(2,1)S(1)}, bf16[672,512]{1,0:T(8,128)(2,1)S(1)}, u32[]{:S(2)}, u32[]{:S(2)}) %collective-permute-start.26) | collective-permute-done | bytes 688160 | tf_op jit(solution)/shard_map/ppermute | solution.py:706
  319.6 5.4 %collective-permute-start.41 = (bf16[256,512]{1,0:T(8,128)(2,1)S(1)}, bf16[256,512]{1,0:T(8,128)(2,1)S(1)}, u32[]{:S(2)}, u32[]{:S(2)}) collective-permute-start(bf16[256,512]{1,0:T(8,128)(2,1)S(1)} %get-tuple-element.189), channel_id=1, source_target_pairs={{0,16},{1,17},{2,18},{3,19},{4,20},{5,21},{6,22},{7,23},{8,24},{9,... | collective-permute-start | bytes 786440 | tf_op jit(solution)/shard_map/ppermute | solution.py:706
  332.2 20.0 %collective-permute-done.41 = bf16[256,512]{1,0:T(8,128)(2,1)S(1)} collective-permute-done((bf16[256,512]{1,0:T(8,128)(2,1)S(1)}, bf16[256,512]{1,0:T(8,128)(2,1)S(1)}, u32[]{:S(2)}, u32[]{:S(2)}) %collective-permute-start.41) | collective-permute-done | bytes 262176 | tf_op jit(solution)/shard_map/ppermute | solution.py:706
  353.2 9.9 %collective-permute-done.31 = bf16[240,512]{1,0:T(8,128)(2,1)S(1)} collective-permute-done((bf16[240,512]{1,0:T(8,128)(2,1)S(1)}, bf16[240,512]{1,0:T(8,128)(2,1)S(1)}, u32[]{:S(2)}, u32[]{:S(2)}) %collective-permute-start.31) | collective-permute-done | bytes 245792 | tf_op jit(solution)/shard_map/ppermute | solution.py:706
  (294 shorter events, 125.0 us)
Async XLA Ops:
  2.6 41.8 %collective-permute-start.15 = (bf16[256,512]{1,0:T(8,128)(2,1)S(1)}, bf16[256,512]{1,0:T(8,128)(2,1)S(1)}, u32[]{:S(2)}, u32[]{:S(2)}) collective-permute-start(bf16[256,512]{1,0:T(8,128)(2,1)S(1)} %constant_dynamic-update-slice_fusion), channel_id=1, source_target_pairs={{0,16},{1,17},{2,18},{3,19},{4,20},{5,21},{6,22},{7,23},{8,24},{9,... | collective-permute-start | bytes 786440 | tf_op jit(solution)/shard_map/ppermute | solution.py:706
  6.7 39.3 %collective-permute-start.16 = (bf16[256,512]{1,0:T(8,128)(2,1)S(1)}, bf16[256,512]{1,0:T(8,128)(2,1)S(1)}, u32[]{:S(2)}, u32[]{:S(2)}) collective-permute-start(bf16[256,512]{1,0:T(8,128)(2,1)S(1)} %constant_dynamic-update-slice_fusion), channel_id=1, source_target_pairs={{0,24},{1,25},{2,26},{3,27},{4,28},{5,29},{6,30},{7,31},{8,16},{9,... | collective-permute-start | bytes 786440 | tf_op jit(solution)/shard_map/ppermute | solution.py:706
  17.1 25.3 %collective-permute-start.6 = (bf16[176,512]{1,0:T(8,128)(2,1)S(1)}, bf16[176,512]{1,0:T(8,128)(2,1)S(1)}, u32[]{:S(2)}, u32[]{:S(2)}) collective-permute-start(bf16[176,512]{1,0:T(8,128)(2,1)S(1)} %get-tuple-element.210), channel_id=1, source_target_pairs={{0,16},{1,17},{2,18},{3,19},{4,20},{5,21},{6,22},{7,23},{8,24},{9,... | collective-permute-start | bytes 540680 | tf_op jit(solution)/shard_map/ppermute | solution.py:706
  18.8 23.5 %collective-permute-start.7 = (bf16[176,512]{1,0:T(8,128)(2,1)S(1)}, bf16[176,512]{1,0:T(8,128)(2,1)S(1)}, u32[]{:S(2)}, u32[]{:S(2)}) collective-permute-start(bf16[176,512]{1,0:T(8,128)(2,1)S(1)} %get-tuple-element.210), channel_id=1, source_target_pairs={{0,24},{1,25},{2,26},{3,27},{4,28},{5,29},{6,30},{7,31},{8,16},{9,... | collective-permute-start | bytes 540680 | tf_op jit(solution)/shard_map/ppermute | solution.py:706
  19.7 22.7 %collective-permute-start.3 = (bf16[176,512]{1,0:T(8,128)(2,1)S(1)}, bf16[176,512]{1,0:T(8,128)(2,1)S(1)}, u32[]{:S(2)}, u32[]{:S(2)}) collective-permute-start(bf16[176,512]{1,0:T(8,128)(2,1)S(1)} %get-tuple-element.210), channel_id=1, source_target_pairs={{0,8},{1,9},{2,10},{3,11},{4,12},{5,13},{6,14},{7,15},{8,0},{9,1},... | collective-permute-start | bytes 540680 | tf_op jit(solution)/shard_map/ppermute | solution.py:706
  42.3 26.3 %collective-permute-start = (bf16[512,1024]{1,0:T(8,128)(2,1)S(1)}, bf16[512,1024]{1,0:T(8,128)(2,1)S(1)}, u32[]{:S(2)}, u32[]{:S(2)}) collective-permute-start(bf16[512,1024]{1,0:T(8,128)(2,1)S(1)} %fusion.3), channel_id=1, source_target_pairs={{0,1},{1,0},{2,3},{3,2},{4,5},{5,4},{6,7},{7,6},{8,9},{9,8},{10,11... | collective-permute-start | bytes 3145736 | tf_op jit(solution)/shard_map/ppermute | solution.py:706
  54.6 27.9 %collective-permute-start.9 = (bf16[2,2,176,512]{3,2,1,0:T(8,128)(2,1)}, bf16[2,2,176,512]{3,2,1,0:T(8,128)(2,1)}, u32[]{:S(2)}, u32[]{:S(2)}) collective-permute-start(bf16[2,2,176,512]{3,2,1,0:T(8,128)(2,1)} %pad_maximum_fusion.4.p2), channel_id=1, source_target_pairs={{0,4},{1,5},{2,6},{3,7},{4,0},{5,1},{6,2},{7,3},{8,12},{9,13},{10,... | collective-permute-start | bytes 2162696 | tf_op jit(solution)/shard_map/ppermute | solution.py:706
  57.5 25.1 %collective-permute-start.5 = (bf16[2,2,176,512]{3,2,1,0:T(8,128)(2,1)}, bf16[2,2,176,512]{3,2,1,0:T(8,128)(2,1)}, u32[]{:S(2)}, u32[]{:S(2)}) collective-permute-start(bf16[2,2,176,512]{3,2,1,0:T(8,128)(2,1)} %pad_maximum_fusion.3.p0), channel_id=1, source_target_pairs={{0,2},{1,3},{2,0},{3,1},{4,6},{5,7},{6,4},{7,5},{8,10},{9,11},{10,... | collective-permute-start | bytes 2162696 | tf_op jit(solution)/shard_map/ppermute | solution.py:706
  65.0 75.0 %collective-permute-start.18 = (bf16[2,2,256,512]{3,2,1,0:T(8,128)(2,1)S(1)}, bf16[2,2,256,512]{3,2,1,0:T(8,128)(2,1)}, u32[]{:S(2)}, u32[]{:S(2)}) collective-permute-start(bf16[2,2,256,512]{3,2,1,0:T(8,128)(2,1)S(1)} %pad_maximum_fusion.2.p2), channel_id=1, source_target_pairs={{0,4},{1,5},{2,6},{3,7},{4,0},{5,1},{6,2},{7,3},{8,12},{9,13},{10,... | collective-permute-start | bytes 3145736 | tf_op jit(solution)/shard_map/ppermute | solution.py:706
  67.1 73.0 %collective-permute-start.14 = (bf16[2,2,256,512]{3,2,1,0:T(8,128)(2,1)S(1)}, bf16[2,2,256,512]{3,2,1,0:T(8,128)(2,1)}, u32[]{:S(2)}, u32[]{:S(2)}) collective-permute-start(bf16[2,2,256,512]{3,2,1,0:T(8,128)(2,1)S(1)} %pad_maximum_fusion.1.p0), channel_id=1, source_target_pairs={{0,2},{1,3},{2,0},{3,1},{4,6},{5,7},{6,4},{7,5},{8,10},{9,11},{10,... | collective-permute-start | bytes 3145736 | tf_op jit(solution)/shard_map/ppermute | solution.py:706
  71.1 31.5 %collective-permute-start.1 = (bf16[16,1024]{1,0:T(8,128)(2,1)S(1)}, bf16[16,1024]{1,0:T(8,128)(2,1)S(1)}, u32[]{:S(2)}, u32[]{:S(2)}) collective-permute-start(bf16[16,1024]{1,0:T(8,128)(2,1)S(1)} %slice.378), channel_id=1, source_target_pairs={{0,2},{1,3},{4,6},{5,7},{8,10},{9,11},{12,14},{13,15},{16,18},{17,... | collective-permute-start | bytes 98312 | tf_op jit(solution)/shard_map/ppermute | solution.py:710
  193.3 24.5 %collective-permute-start.23 = (bf16[128,1024]{1,0:T(8,128)(2,1)S(1)}, bf16[128,1024]{1,0:T(8,128)(2,1)S(1)}, u32[]{:S(2)}, u32[]{:S(2)}) collective-permute-start(bf16[128,1024]{1,0:T(8,128)(2,1)S(1)} %convert_element_type.279), channel_id=1, source_target_pairs={{2,0},{3,1},{6,4},{7,5},{10,8},{11,9},{14,12},{15,13},{18,16},{19,... | collective-permute-start | bytes 786440 | tf_op jit(solution)/shard_map/ppermute | solution.py:714
  213.6 76.3 %collective-permute-start.36 = (bf16[2,2,256,512]{3,2,0,1:T(8,128)(2,1)}, bf16[2,2,256,512]{3,2,0,1:T(8,128)(2,1)}, u32[]{:S(2)}, u32[]{:S(2)}) collective-permute-start(bf16[2,2,256,512]{3,2,0,1:T(8,128)(2,1)} %copy.58), channel_id=1, source_target_pairs={{0,2},{1,3},{2,0},{3,1},{4,6},{5,7},{6,4},{7,5},{8,10},{9,11},{10,... | collective-permute-start | bytes 3145736 | tf_op jit(solution)/shard_map/ppermute | solution.py:706
  216.2 76.9 %collective-permute-start.39 = (bf16[2,2,256,512]{3,2,1,0:T(8,128)(2,1)}, bf16[2,2,256,512]{3,2,1,0:T(8,128)(2,1)}, u32[]{:S(2)}, u32[]{:S(2)}) collective-permute-start(bf16[2,2,256,512]{3,2,1,0:T(8,128)(2,1)} %get-tuple-element.148), channel_id=1, source_target_pairs={{0,4},{1,5},{2,6},{3,7},{4,0},{5,1},{6,2},{7,3},{8,12},{9,13},{10,... | collective-permute-start | bytes 3145736 | tf_op jit(solution)/shard_map/ppermute | solution.py:706
  250.8 22.2 %collective-permute-start.24 = (bf16[1024,256]{1,0:T(8,128)(2,1)}, bf16[1024,256]{1,0:T(8,128)(2,1)S(1)}, u32[]{:S(2)}, u32[]{:S(2)}) collective-permute-start(bf16[1024,256]{1,0:T(8,128)(2,1)} %get-tuple-element.128.dbc_ref), channel_id=1, source_target_pairs={{0,1},{1,0},{2,3},{3,2},{4,5},{5,4},{6,7},{7,6},{8,9},{9,8},{10,11... | collective-permute-start | bytes 1572872 | tf_op jit(solution)/shard_map/ppermute | solution.py:706
  272.9 24.0 %collective-permute-start.35 = (bf16[512,1024]{1,0:T(8,128)(2,1)}, bf16[512,1024]{1,0:T(8,128)(2,1)S(1)}, u32[]{:S(2)}, u32[]{:S(2)}) collective-permute-start(bf16[512,1024]{1,0:T(8,128)(2,1)} %get-tuple-element.144), channel_id=1, source_target_pairs={{0,1},{1,0},{2,3},{3,2},{4,5},{5,4},{6,7},{7,6},{8,9},{9,8},{10,11... | collective-permute-start | bytes 3145736 | tf_op jit(solution)/shard_map/ppermute | solution.py:706
  291.6 20.6 %collective-permute-start.37 = (bf16[2,256,512]{2,1,0:T(8,128)(2,1)S(1)}, bf16[2,256,512]{2,1,0:T(8,128)(2,1)S(1)}, u32[]{:S(2)}, u32[]{:S(2)}) collective-permute-start(bf16[2,256,512]{2,1,0:T(8,128)(2,1)S(1)} %slice_bitcast_fusion.2), channel_id=1, source_target_pairs={{0,4},{1,5},{2,6},{3,7},{4,0},{5,1},{6,2},{7,3},{8,12},{9,13},{10,... | collective-permute-start | bytes 1572872 | tf_op jit(solution)/shard_map/ppermute | solution.py:706
  294.9 24.5 %collective-permute-start.40 = (bf16[2,256,512]{2,1,0:T(8,128)(2,1)S(1)}, bf16[2,256,512]{2,1,0:T(8,128)(2,1)S(1)}, u32[]{:S(2)}, u32[]{:S(2)}) collective-permute-start(bf16[2,256,512]{2,1,0:T(8,128)(2,1)S(1)} %slice_bitcast_fusion), channel_id=1, source_target_pairs={{0,2},{1,3},{2,0},{3,1},{4,6},{5,7},{6,4},{7,5},{8,10},{9,11},{10,... | collective-permute-start | bytes 1572872 | tf_op jit(solution)/shard_map/ppermute | solution.py:706
  301.2 24.2 %collective-permute-start.30 = (bf16[2,144,512]{2,1,0:T(8,128)(2,1)S(1)}, bf16[2,144,512]{2,1,0:T(8,128)(2,1)S(1)}, u32[]{:S(2)}, u32[]{:S(2)}) collective-permute-start(bf16[2,144,512]{2,1,0:T(8,128)(2,1)S(1)} %slice_bitcast_fusion.4), channel_id=1, source_target_pairs={{0,2},{1,3},{2,0},{3,1},{4,6},{5,7},{6,4},{7,5},{8,10},{9,11},{10,... | collective-permute-start | bytes 884744 | tf_op jit(solution)/shard_map/ppermute | solution.py:706
  319.6 32.7 %collective-permute-start.41 = (bf16[256,512]{1,0:T(8,128)(2,1)S(1)}, bf16[256,512]{1,0:T(8,128)(2,1)S(1)}, u32[]{:S(2)}, u32[]{:S(2)}) collective-permute-start(bf16[256,512]{1,0:T(8,128)(2,1)S(1)} %get-tuple-element.189), channel_id=1, source_target_pairs={{0,16},{1,17},{2,18},{3,19},{4,20},{5,21},{6,22},{7,23},{8,24},{9,... | collective-permute-start | bytes 786440 | tf_op jit(solution)/shard_map/ppermute | solution.py:706
  324.9 27.3 %collective-permute-start.42 = (bf16[256,512]{1,0:T(8,128)(2,1)S(1)}, bf16[256,512]{1,0:T(8,128)(2,1)S(1)}, u32[]{:S(2)}, u32[]{:S(2)}) collective-permute-start(bf16[256,512]{1,0:T(8,128)(2,1)S(1)} %get-tuple-element.190), channel_id=1, source_target_pairs={{0,24},{1,25},{2,26},{3,27},{4,28},{5,29},{6,30},{7,31},{8,16},{9,... | collective-permute-start | bytes 786440 | tf_op jit(solution)/shard_map/ppermute | solution.py:706
  325.8 27.4 %collective-permute-start.28 = (bf16[240,512]{1,0:T(8,128)(2,1)S(1)}, bf16[240,512]{1,0:T(8,128)(2,1)S(1)}, u32[]{:S(2)}, u32[]{:S(2)}) collective-permute-start(bf16[240,512]{1,0:T(8,128)(2,1)S(1)} %get-tuple-element.214), channel_id=1, source_target_pairs={{0,8},{1,9},{2,10},{3,11},{4,12},{5,13},{6,14},{7,15},{8,0},{9,1},... | collective-permute-start | bytes 737288 | tf_op jit(solution)/shard_map/ppermute | solution.py:706
  328.8 34.3 %collective-permute-start.31 = (bf16[240,512]{1,0:T(8,128)(2,1)S(1)}, bf16[240,512]{1,0:T(8,128)(2,1)S(1)}, u32[]{:S(2)}, u32[]{:S(2)}) collective-permute-start(bf16[240,512]{1,0:T(8,128)(2,1)S(1)} %get-tuple-element.215), channel_id=1, source_target_pairs={{0,16},{1,17},{2,18},{3,19},{4,20},{5,21},{6,22},{7,23},{8,24},{9,... | collective-permute-start | bytes 737288 | tf_op jit(solution)/shard_map/ppermute | solution.py:706
  330.8 32.3 %collective-permute-start.32 = (bf16[240,512]{1,0:T(8,128)(2,1)S(1)}, bf16[240,512]{1,0:T(8,128)(2,1)S(1)}, u32[]{:S(2)}, u32[]{:S(2)}) collective-permute-start(bf16[240,512]{1,0:T(8,128)(2,1)S(1)} %get-tuple-element.216), channel_id=1, source_target_pairs={{0,24},{1,25},{2,26},{3,27},{4,28},{5,29},{6,30},{7,31},{8,16},{9,... | collective-permute-start | bytes 737288 | tf_op jit(solution)/shard_map/ppermute | solution.py:706
  (53 other events, 411.6 us)
